TPU v7x, 32 devices: a whole 2x2x4 slice. The times are simulated.
32 devices in a mesh: role: 4 (over x, core), fsdp: 4 (over z), tp: 2 (over y).
Axes of the slice: x: 2, y: 2, z: 4, core: 2. Of those that a mesh axis runs over, the one named last changes fastest.
Arguments:
- master: float32 [5120, 2, 1024], P(('role', 'fsdp', 'tp')), may hold values from -0.078125 to 0.078125
- gradient: float32 [5120, 2, 1024], P(('role', 'fsdp', 'tp')), may hold values from -6 to 6
- first_moment: float32 [5120, 2, 1024], P(('role', 'fsdp', 'tp')), may hold values from -3 to 3
- second_moment: float32 [5120, 2, 1024], P(('role', 'fsdp', 'tp')), may hold values from 0.001 to 1
- key_gain: bfloat16 [128], replicated, may hold values from 0.099609375 to 1.8984375
- hidden: bfloat16 [64, 48, 5120], P(('role', 'fsdp')), may hold values from -6 to 6
- queries: bfloat16 [64, 48, 64, 128], P(('role', 'fsdp'), None, 'tp'), may hold values from -160 to 160
- key_cache: bfloat16 [64, 8, 192, 128], P(('role', 'fsdp'), 'tp'), may hold values from -6 to 6
- value_cache: bfloat16 [64, 8, 192, 128], P(('role', 'fsdp'), 'tp'), may hold values from -6 to 6
- cache_lengths: int32 [64], P(('role', 'fsdp')), may hold values from 2 to 192, as said below
- tool_lengths: int32 [64], P(('role', 'fsdp')), may hold values from 1 to 48, as said below
Outputs:
- updated_master: float32 [5120, 2, 1024], P(('role', 'fsdp', 'tp'))
- updated_first: float32 [5120, 2, 1024], P(('role', 'fsdp', 'tp'))
- updated_second: float32 [5120, 2, 1024], P(('role', 'fsdp', 'tp'))
- new_entries: bfloat16 [64, 48, 2, 1024], P(('role', 'fsdp'), None, None, 'tp')
- attended: bfloat16 [64, 48, 64, 128], P(('role', 'fsdp'), None, 'tp')
Inputs may be any that keep to these rules, and one draw needn't show every extreme that they name: `cache_lengths`: one sequence in every draw has exactly 192 filled slots. `tool_lengths`: one sequence in every draw has a tool result of exactly 48 tokens.
All inputs are finite; a program needn't handle non-finite values.
Results may differ from a plain program's by a relative error of at most 0.0059.
Values may be sent and summed in bfloat16 or wider, within the bound.
No kernel may reach another device: no remote copies, remote signals or barrier semaphores. Data moves between devices by JAX's collectives and lax.ppermute only.
A program may use at most 64 MiB of HBM per device.

v0:
```python
import math

import jax
import jax.numpy as jnp
from jax import lax
from jax.sharding import PartitionSpec as P

learn_rate = 0.01
decay_rate = 0.1
bias_first = 1.0 - 0.9**10
bias_second = 1.0 - 0.95**10
rope_theta = 1000000.0


def adam_update(master, gradient, first_moment, second_moment):
    moment_one = 0.9 * first_moment + 0.1 * gradient
    moment_two = 0.95 * second_moment + 0.05 * gradient * gradient
    step_size = moment_one / bias_first / (jnp.sqrt(moment_two / bias_second) + 1e-08)
    updated = master * (1.0 - learn_rate * decay_rate) - learn_rate * step_size
    return (updated, moment_one, moment_two)


def rotate_keys(raw_keys, positions, key_gain):
    head_size = raw_keys.shape[-1]
    half_size = head_size // 2
    normed = raw_keys / jnp.sqrt(jnp.mean(raw_keys * raw_keys, axis=-1, keepdims=True) + 1e-06)
    normed = normed * key_gain.astype(jnp.float32)
    inverse = rope_theta ** (-(jnp.arange(half_size, dtype=jnp.float32) * 2.0) / head_size)
    angles = positions.astype(jnp.float32)[:, :, None] * inverse[None, None, :]
    cosine = jnp.cos(angles)[:, :, None, :]
    sine_part = jnp.sin(angles)[:, :, None, :]
    lower_half = normed[..., :half_size]
    upper_half = normed[..., half_size:]
    return jnp.concatenate(
        [
            lower_half * cosine - upper_half * sine_part,
            upper_half * cosine + lower_half * sine_part,
        ],
        axis=-1,
    )


def attend(queries, key_cache, value_cache, new_keys, new_values, cache_lengths, tool_lengths):
    sequences, new_rows, qheads, head_size = queries.shape
    groups = key_cache.shape[1]
    cache_size = key_cache.shape[2]
    grouped = queries.reshape(sequences, new_rows, groups, qheads // groups, head_size)
    score_scale = 1.0 / math.sqrt(head_size)
    cache_score = (
        jnp.einsum("srgah,sgch->sgarc", grouped, key_cache, preferred_element_type=jnp.float32)
        * score_scale
    )
    new_score = (
        jnp.einsum("srgah,sugh->sgaru", grouped, new_keys, preferred_element_type=jnp.float32)
        * score_scale
    )
    cache_mask = (jnp.arange(cache_size, dtype=jnp.int32)[None, :] < cache_lengths[:, None])[
        :, None, None, None, :
    ]
    causal_mask = (
        jnp.arange(new_rows, dtype=jnp.int32)[None, :]
        <= jnp.arange(new_rows, dtype=jnp.int32)[:, None]
    )[None, None, None, :, :]
    cache_score = jnp.where(cache_mask, cache_score, -1e30)
    new_score = jnp.where(causal_mask, new_score, -1e30)
    row_max = jnp.maximum(jnp.max(cache_score, axis=-1), jnp.max(new_score, axis=-1))
    cache_exp = jnp.exp(cache_score - row_max[..., None])
    new_exp = jnp.exp(new_score - row_max[..., None])
    denominator = jnp.sum(cache_exp, axis=-1) + jnp.sum(new_exp, axis=-1)
    cache_prob = cache_exp.astype(jnp.bfloat16)
    new_prob = new_exp.astype(jnp.bfloat16)
    mixed = jnp.einsum(
        "sgarc,sgch->sgarh", cache_prob, value_cache, preferred_element_type=jnp.float32
    )
    mixed = mixed + jnp.einsum(
        "sgaru,sugh->sgarh", new_prob, new_values, preferred_element_type=jnp.float32
    )
    result = mixed / denominator[..., None]
    result = jnp.transpose(result, (0, 3, 1, 2, 4)).reshape(sequences, new_rows, qheads, head_size)
    live_rows = (jnp.arange(new_rows, dtype=jnp.int32)[None, :] < tool_lengths[:, None])[
        :, :, None, None
    ]
    return jnp.where(live_rows, result, 0.0).astype(jnp.bfloat16)


def per_device(
    master,
    gradient,
    first_moment,
    second_moment,
    key_gain,
    hidden,
    queries,
    key_cache,
    value_cache,
    cache_lengths,
    tool_lengths,
):
    updated, moment_one, moment_two = adam_update(master, gradient, first_moment, second_moment)
    weights = updated.astype(jnp.bfloat16)
    sequences, new_rows, model_width = hidden.shape
    row_count = sequences * new_rows
    tokens = hidden.reshape(row_count, model_width)
    groups = key_cache.shape[1]
    head_size = key_cache.shape[3]
    kv_cols = groups * head_size
    tp_count = lax.axis_size("tp")
    own_rows = weights.shape[0]
    split_view = tokens.reshape(row_count, model_width // (tp_count * own_rows), tp_count, own_rows)
    picked = lax.dynamic_slice_in_dim(split_view, lax.axis_index("tp"), 1, 2).reshape(row_count, -1)
    tp_rows = lax.all_gather(weights, ("role", "fsdp"), axis=0, tiled=True)
    partial_value = jnp.dot(
        picked, tp_rows.reshape(tp_rows.shape[0], -1), preferred_element_type=jnp.float32
    )
    projected = lax.psum_scatter(
        partial_value.reshape(row_count, 2, weights.shape[2]), "tp", scatter_dimension=2, tiled=True
    )
    projected = projected.reshape(sequences, new_rows, 2, groups, head_size)
    positions = cache_lengths[:, None] + jnp.arange(new_rows, dtype=jnp.int32)[None, :]
    new_keys = rotate_keys(projected[:, :, 0], positions, key_gain).astype(jnp.bfloat16)
    new_values = projected[:, :, 1].astype(jnp.bfloat16)
    new_entries = jnp.stack(
        [
            new_keys.reshape(sequences, new_rows, kv_cols),
            new_values.reshape(sequences, new_rows, kv_cols),
        ],
        axis=2,
    )
    attended = attend(
        queries, key_cache, value_cache, new_keys, new_values, cache_lengths, tool_lengths
    )
    return (updated, moment_one, moment_two, new_entries, attended)


def solution(mesh):
    return jax.shard_map(
        per_device,
        mesh=mesh,
        in_specs=(
            P(("role", "fsdp", "tp"), None, None),
            P(("role", "fsdp", "tp"), None, None),
            P(("role", "fsdp", "tp"), None, None),
            P(("role", "fsdp", "tp"), None, None),
            P(),
            P(("role", "fsdp"), None, None),
            P(("role", "fsdp"), None, "tp", None),
            P(("role", "fsdp"), "tp", None, None),
            P(("role", "fsdp"), "tp", None, None),
            P(("role", "fsdp")),
            P(("role", "fsdp")),
        ),
        out_specs=(
            P(("role", "fsdp", "tp"), None, None),
            P(("role", "fsdp", "tp"), None, None),
            P(("role", "fsdp", "tp"), None, None),
            P(("role", "fsdp"), None, None, "tp"),
            P(("role", "fsdp"), None, "tp", None),
        ),
        check_vma=False,
    )
```

profile of v0, /device:TPU:0, one launch (start us, length us, event | category | flops | bytes accessed | tf_op | source)
XLA Modules:
  0.0 186.5 jit_solution(5282786478064503759)
XLA Ops:
  7.2 7.8 %fusion.34 = (bf16[160,2,1024]{2,1,0:T(2,128)(2,1)}, f32[160,2,1024]{2,1,0:T(2,128)}, f32[160,2,1024]{2,1,0:T(2,128)}, f32[160,2,1024]{2,1,0:T(2,128)}) fusion(f32[160,2,1024]{2,1,0:T(2,128)} %param.11, f32[160,2,1024]{2,1,0:T(2,128)} %param.12, f32[160,2,1024]{2,1,0:T(2,128)} %param.13, f32[160,2,1024]{2,1,0:T(2,128)} %param.14), kind=kLoop, calls=%fused_computation.62 | loop fusion | flops 4915200 | bytes 9830400 | tf_op jit(solution)/shard_map/convert_element_type | solution.py:100
  15.2 4.7 %reshape_reshape.3 = bf16[192,16,2,160]{3,2,1,0:T(2,128)(2,1)} reshape(bf16[4,48,5120]{2,1,0:T(8,128)(2,1)S(1)} %copy-done.2) | data formatting | bytes 3932160 | tf_op jit(solution)/shard_map/reshape;reshape | solution.py:109
  19.8 7.4 %constant_dynamic-slice_fusion = bf16[192,16,1,160]{3,2,1,0:T(2,128)(2,1)} fusion(bf16[192,16,2,160]{3,2,1,0:T(2,128)(2,1)} %reshape_reshape.3, s32[]{:T(128)S(6)} %select_n.18), kind=kLoop, calls=%fused_computation.57 | loop fusion | bytes 1966084 | tf_op jit(solution)/shard_map/dynamic_slice | solution.py:110
  27.3 7.8 %copy.36 = bf16[192,16,1,160]{0,3,1,2:T(8,128)(2,1)S(1)} copy(bf16[192,16,1,160]{3,2,1,0:T(2,128)(2,1)} %constant_dynamic-slice_fusion) | data formatting | bytes 1966080 | tf_op jit(solution)/shard_map/dynamic_slice | solution.py:110
  35.1 70.8 %all-gather.2.cloned.1.call-done = bf16[2560,2,1024]{2,1,0:T(2,128)(2,1)} async-done(((bf16[160,2,1024]{2,1,0:T(2,128)(2,1)}), bf16[2560,2,1024]{2,1,0:T(2,128)(2,1)}) %all-gather.2.cloned.1.call-update) | async-done | bytes 10485776 | tf_op jit(solution)/shard_map/all_gather | solution.py:111
  105.8 26.2 %copy.55 = bf16[2560,2,1024]{0,2,1:T(8,128)(2,1)} copy(bf16[2560,2,1024]{2,1,0:T(2,128)(2,1)} %all-gather.2.cloned.1.call-done) | data formatting | bytes 20971520 | tf_op jit(solution)/shard_map/reshape | solution.py:113
  132.0 8.8 %fusion = f32[192,2,1024]{2,0,1:T(8,128)} fusion(bf16[192,2560,1]{0,1,2:T(8,128)(2,1)S(1)} %bitcast.76, bf16[2560,2,1024]{0,2,1:T(8,128)(2,1)} %copy.55), kind=kOutput, calls=%fused_computation | convolution fusion | flops 2013265920 | bytes 13041664 | tf_op jit(solution)/shard_map/dot_general | solution.py:112
  141.1 0.4 multiply_cosine_fusion
  141.6 5.3 %bitcast_reduce_fusion = (f32[4,4,8,48]{3,2,1,0:T(8,128)S(1)}, f32[4,4,192,48,8]{2,3,4,1,0:T(8,128)}) fusion(pred[4,192]{1,0:T(4,128)(4,1)S(1)} %iota_compare_fusion.1, bf16[4,48,4,8,128]{4,3,2,1,0:T(8,128)(2,1)S(1)} %bitcast.74, bf16[4,4,192,128]{3,2,1,0:T(8,128)(2,1)} %param.18), kind=kOutput, calls=%fused_computation.3 | convolution fusion | flops 305522688 | bytes 7103232 | tf_op jit(solution)/shard_map/srgah,sgch->sgarc/dot_general | solution.py:50
  146.8 18.4 %reduce-scatter.2.cloned.1.call-done = f32[192,2,512]{2,0,1:T(8,128)} async-done(((f32[192,2,1024]{2,0,1:T(8,128)}), f32[192,2,512]{2,0,1:T(8,128)}) %reduce-scatter.2.cloned.1.call-update) | async-done | bytes 786448 | tf_op jit(solution)/shard_map/reduce_scatter | solution.py:115
  165.2 1.4 reshape.151
  166.8 0.2 multiply_reduce_fusion
  167.0 0.2 divide_multiply_fusion
  167.2 0.2 multiply_subtract_fusion.1
  167.4 0.1 maximum_convert_fusion
  167.5 0.1 copy.40
  167.6 0.1 convert_element_type.55
  167.7 1.2 copy.47
  168.9 2.0 %fusion.14 = (f32[4,4,8,48]{3,2,1,0:T(8,128)S(1)}, f32[4,4,48,48,8]{3,2,4,1,0:T(8,128)S(1)}) fusion(pred[48,48]{0,1:T(8,128)(4,1)S(1)} %iota_compare_fusion, bf16[4,48,4,8,128]{4,3,2,1,0:T(8,128)(2,1)S(1)} %bitcast.75, bf16[4,48,4,128]{3,1,2,0:T(8,128)(2,1)S(1)} %maximum_convert_fusion), kind=kOutput, calls=%fused_computation.20 | convolution fusion | flops 76376064 | bytes 2976000 | tf_op jit(solution)/shard_map/srgah,sugh->sgaru/dot_general | solution.py:54
  170.9 2.3 %fusion.3 = f32[4,4,8,48]{3,2,1,0:T(8,128)S(1)} fusion(f32[4,4,192,48,8]{2,3,4,1,0:T(8,128)S(1)} %copy-done.1, f32[4,4,8,48]{3,2,1,0:T(8,128)S(1)} %max.7, pred[4,192]{1,0:T(4,128)(4,1)S(1)} %iota_compare_fusion.1), kind=kLoop, calls=%fused_computation.6 | loop fusion | flops 4712448 | bytes 4768512 | tf_op jit(solution)/shard_map/reduce_sum | solution.py:69
  173.2 2.0 %fusion.5 = f32[4,4,8,48,128]{4,3,2,1,0:T(8,128)S(1)} fusion(f32[4,4,192,48,8]{2,3,4,1,0:T(8,128)S(1)} %copy-done.1, f32[4,4,8,48]{3,2,1,0:T(8,128)S(1)} %max.7, pred[4,192]{1,0:T(4,128)(4,1)S(1)} %iota_compare_fusion.1, bf16[4,4,192,128]{3,2,1,0:T(8,128)(2,1)S(1)} %copy-done.4), kind=kOutput, calls=%fused_computation.8 | convolution fusion | flops 306708480 | bytes 8676096 | tf_op jit(solution)/shard_map/sgarc,sgch->sgarh/dot_general | solution.py:72
  175.2 1.1 fusion.12
  176.3 1.8 bitcast_divide_fusion
  178.0 1.6 fusion.7
  (31 shorter events, 0.6 us)
Async XLA Ops:
  7.2 134.4 %copy-start = (bf16[4,48,32,128]{3,2,1,0:T(8,128)(2,1)S(1)}, bf16[4,48,32,128]{3,2,1,0:T(8,128)(2,1)}, u32[]{:S(2)}) copy-start(bf16[4,48,32,128]{3,2,1,0:T(8,128)(2,1)} %param.17) | copy-start | bytes 4718596
  7.2 8.0 %copy-start.2 = (bf16[4,48,5120]{2,1,0:T(8,128)(2,1)S(1)}, bf16[4,48,5120]{2,1,0:T(8,128)(2,1)}, u32[]{:S(2)}) copy-start(bf16[4,48,5120]{2,1,0:T(8,128)(2,1)} %param.16) | copy-start | bytes 5898244
  7.2 98.6 %all-gather.2.cloned.1.call-start = ((), (), s32[]{:S(2)}) async-start(), calls=%async_computation.1 | async-start | bytes 11141120 | tf_op jit(solution)/shard_map/all_gather | solution.py:111
  15.1 150.1 %reduce-scatter.2.cloned.1.call-start = ((), (), s32[]{:S(2)}) async-start(), calls=%async_computation.2 | async-start | bytes 2359296 | tf_op jit(solution)/shard_map/reduce_scatter | solution.py:115
  132.0 8.8 %copy-start.5 = (bf16[128]{0:T(256)(128)(2,1)S(1)}, bf16[128]{0:T(256)(128)(2,1)}, u32[]{:S(2)}) copy-start(bf16[128]{0:T(256)(128)(2,1)} %param.15) | copy-start | bytes 772
  132.0 8.9 %copy-start.6 = (s32[4]{0:T(128)S(1)}, s32[4]{0:T(128)}, u32[]{:S(2)}) copy-start(s32[4]{0:T(128)} %param.21) | copy-start | bytes 52
  132.0 9.0 %copy-start.3 = (s32[4]{0:T(128)S(1)}, s32[4]{0:T(128)}, u32[]{:S(2)}) copy-start(s32[4]{0:T(128)} %param.20) | copy-start | bytes 52
  167.7 3.2 %copy-start.1 = (f32[4,4,192,48,8]{2,3,4,1,0:T(8,128)S(1)}, f32[4,4,192,48,8]{2,3,4,1,0:T(8,128)}, u32[]{:S(2)}) copy-start(f32[4,4,192,48,8]{2,3,4,1,0:T(8,128)} %get-tuple-element.24) | copy-start | bytes 14155780
  170.9 2.3 %copy-start.4 = (bf16[4,4,192,128]{3,2,1,0:T(8,128)(2,1)S(1)}, bf16[4,4,192,128]{3,2,1,0:T(8,128)(2,1)}, u32[]{:S(2)}) copy-start(bf16[4,4,192,128]{3,2,1,0:T(8,128)(2,1)} %param.19) | copy-start | bytes 2359300
Sparse Core Ops, SparseCore 0:
  15.2 90.5 all-gather.1
  141.0 24.2 reduce-scatter.1
where the time goes:
time: 188 us; the launch traced here: 187 us
  waiting for transfers between devices  89.2 us (47%)
  local copies, waits for them, and re-layouts  48.9 us (26%)
  matrix products  19.8 us (11%)
  between operations  14.3 us (8%)
  other arithmetic  14.2 us (8%)
    all_gather x1, waiting for transfers between devices, per_device(): tp_rows = lax.all_gather(weights, ('role', 'fsdp'), axis=0, tiled=True)  70.8 us
    reshape x1, local copies, waits for them, and re-layouts, per_device(): tp_rows.reshape(tp_rows.shape[0], -1)  26.2 us
    reduce_scatter x1, waiting for transfers between devices, per_device(): lax.psum_scatter(partial_value.reshape(row_count, 2, weights.shape[2]), '...  18.4 us
    dynamic_slice x2, local copies, waits for them, and re-layouts, per_device(): lax.dynamic_slice_in_dim(split_view, lax.axis_index('tp'), 1, 2)  15.2 us
    dot_general x1, matrix products, per_device(): jnp.dot(picked, tp_rows.reshape(tp_rows.shape[0], -1), preferred_element_...  8.81 us
    convert_element_type x1, other arithmetic, per_device(): weights = updated.astype(jnp.bfloat16)  7.82 us
    dot_general x1, matrix products, attend(): jnp.einsum('srgah,sgch->sgarc', grouped, key_cache, preferred_element_typ...  5.28 us
    another operation x1, local copies, waits for them, and re-layouts, per_device(): tokens.reshape(row_count, model_width // (tp_count * own_rows), tp_count,...  4.69 us
  transfers between devices with their start and end apart: 2, of which 2 were waited for; matrix products, arithmetic and copies ran while one was open for 14% of the time, Pallas kernels for 0%

commit v1 on v0

--- a/solution.py
+++ b/solution.py
@@ -1,8 +1,11 @@
+import functools
 import math
 
 import jax
 import jax.numpy as jnp
 from jax import lax
+from jax.experimental import pallas as pl
+from jax.experimental.pallas import tpu as pltpu
 from jax.sharding import PartitionSpec as P
 
 learn_rate = 0.01
@@ -83,7 +86,7 @@
     return jnp.where(live_rows, result, 0.0).astype(jnp.bfloat16)
 
 
-def per_device(
+def plain_device(
     master,
     gradient,
     first_moment,
@@ -132,9 +135,349 @@
     return (updated, moment_one, moment_two, new_entries, attended)
 
 
+CORE_SWAP = ((0, 1), (1, 0), (2, 3), (3, 2))
+X_SWAP = ((0, 2), (1, 3), (2, 0), (3, 1))
+DIAGONAL = ((0, 3), (1, 2), (2, 1), (3, 0))
+Z_NEAR = ((0, 1), (1, 0), (2, 3), (3, 2))
+Z_FAR = ((0, 2), (2, 0), (1, 3), (3, 1))
+Z_MIDDLE = ((1, 2), (2, 1))
+Z_ENDS = ((2, 3), (1, 0))
+TP_SWAP = ((0, 1), (1, 0))
+MASKED = -1e30
+
+
+def adam_kernel(head_count, m_ref, g_ref, f_ref, s_ref, um_ref, uf_ref, us_ref, own_ref, other_ref):
+    here = lax.axis_index("tp")
+    gradient = g_ref[...]
+    moment_one = 0.9 * f_ref[...] + 0.1 * gradient
+    moment_two = 0.95 * s_ref[...] + 0.05 * gradient * gradient
+    uf_ref[...] = moment_one
+    us_ref[...] = moment_two
+    scaled = moment_one * (learn_rate / bias_first)
+    root = jnp.sqrt(moment_two * (1.0 / bias_second)) + 1e-08
+    um_ref[...] = m_ref[...] * (1.0 - learn_rate * decay_rate) - scaled / root
+    rows = own_ref.shape[0]
+    stride = um_ref.shape[0] // rows
+    for side, out in ((here, own_ref), (1 - here, other_ref)):
+        for kind in range(2):
+            for head in range(head_count):
+                start = (head_count * side + head) * 2 + kind
+                part = um_ref[pl.ds(start, rows, stride=stride), :]
+                column = (kind * head_count + head) * 128
+                out[:, column : column + 128] = part.astype(jnp.bfloat16)
+
+
+def adam_step(master, gradient, first_moment, second_moment, head_count):
+    rows, kinds, width = master.shape
+    blocks = width // 128
+
+    def linear(array):
+        split = array.reshape(rows, kinds, blocks, 128)
+        return split.transpose(0, 2, 1, 3).reshape(rows * kinds * blocks, 128)
+
+    def back(array):
+        return array.reshape(rows, blocks, kinds, 128).transpose(0, 2, 1, 3).reshape(rows, kinds, width)
+
+    steps = 5
+    step_rows = rows // steps
+    flat_spec = pl.BlockSpec((step_rows * kinds * blocks, 128), lambda i: (i, 0))
+    flat_shape = jax.ShapeDtypeStruct((rows * kinds * blocks, 128), jnp.float32)
+    half = kinds * head_count * 128
+    half_spec = pl.BlockSpec((step_rows, half), lambda i: (i, 0))
+    half_shape = jax.ShapeDtypeStruct((rows, half), jnp.bfloat16)
+    updated, one, two, own, other = pl.pallas_call(
+        functools.partial(adam_kernel, head_count),
+        out_shape=(flat_shape,) * 3 + (half_shape,) * 2,
+        grid=(steps,),
+        in_specs=[flat_spec] * 4,
+        out_specs=(flat_spec,) * 3 + (half_spec,) * 2,
+        cost_estimate=pl.CostEstimate(flops=20 * master.size, bytes_accessed=32 * master.size, transcendentals=0),
+        name="adam",
+    )(linear(master), linear(gradient), linear(first_moment), linear(second_moment))
+    return back(updated), back(one), back(two), own, other
+
+
+def project_kernel(
+    h0, h1, h2, h3, o0, p0, o1, p1, o2, p2, ob, pb, oe, pe, keep_ref, send_ref, held, sems
+):
+    z = lax.axis_index("fsdp")
+    t = lax.axis_index("tp")
+    rows = o0.shape[0]
+    inner = jnp.logical_or(z == 1, z == 2)
+
+    def copy(ref, layer, side, sem):
+        start = pl.multiple_of((layer * 2 + side) * rows, 16)
+        return pltpu.make_async_copy(ref, held.at[pl.ds(start, rows)], sems.at[sem])
+
+    near, far, last = z ^ 1, z ^ 2, z ^ 3
+    copies = [
+        copy(o0, z, t, 0),
+        copy(p0, z, 1 - t, 1),
+        copy(o1, near, t, 2),
+        copy(p1, near, 1 - t, 3),
+        copy(o2, far, t, 4),
+        copy(p2, far, 1 - t, 5),
+    ]
+    for each in copies:
+        each.start()
+
+    @pl.when(inner)
+    def _():
+        copy(ob, last, t, 6).start()
+        copy(pb, last, 1 - t, 7).start()
+
+    @pl.when(jnp.logical_not(inner))
+    def _():
+        copy(oe, last, t, 6).start()
+        copy(pe, last, 1 - t, 7).start()
+
+    for each in copies:
+        each.wait()
+    copy(ob, last, t, 6).wait()
+    copy(pb, last, 1 - t, 7).wait()
+    weights = held[...]
+    send_ref[0] = jnp.dot(h1[...], weights, preferred_element_type=jnp.float32)
+    send_ref[1] = jnp.dot(h3[...], weights, preferred_element_type=jnp.float32)
+    keep_ref[0] = jnp.dot(h0[...], weights, preferred_element_type=jnp.float32)
+    keep_ref[1] = jnp.dot(h2[...], weights, preferred_element_type=jnp.float32)
+
+
+def project(tokens, units):
+    count, depth = tokens[0].shape
+    width = units[0].shape[1]
+    result = jax.ShapeDtypeStruct((2, count, width), jnp.float32)
+    whole = pl.BlockSpec(memory_space=pltpu.VMEM)
+    return pl.pallas_call(
+        project_kernel,
+        out_shape=(result, result),
+        in_specs=[whole] * 4 + [pl.BlockSpec(memory_space=pl.ANY)] * 10,
+        out_specs=(whole, whole),
+        scratch_shapes=[pltpu.VMEM((depth, width), jnp.bfloat16), pltpu.SemaphoreType.DMA((8,))],
+        compiler_params=pltpu.CompilerParams(vmem_limit_bytes=40 * 1024 * 1024),
+        cost_estimate=pl.CostEstimate(
+            flops=8 * count * depth * width, bytes_accessed=16 * count * width + 2 * depth * width, transcendentals=0
+        ),
+        name="project",
+    )(*tokens, *units)
+
+
+def cached_kernel(lengths, q_ref, k_ref, v_ref, out_ref, weight_ref):
+    filled = lengths[pl.program_id(0)]
+    groups, slots, head_size = k_ref.shape
+    new_rows, qheads, _ = q_ref.shape
+    share = qheads // groups
+    rows = new_rows * share
+    scale = 1.0 / math.sqrt(head_size)
+    queries = q_ref[...].astype(jnp.float32)
+    inside = lax.broadcasted_iota(jnp.int32, (rows, slots), 1) < filled
+    lane = lax.broadcasted_iota(jnp.int32, (rows, 128), 1)
+    level = jnp.full((rows, 128), MASKED, jnp.float32)
+    for g in range(groups):
+        asked = queries[:, g * share : (g + 1) * share, :].reshape(rows, head_size).astype(jnp.bfloat16)
+        scores = lax.dot_general(
+            asked, k_ref[g], (((1,), (1,)), ((), ())), preferred_element_type=jnp.float32
+        )
+        scores = jnp.where(inside, scores * scale, MASKED)
+        top = jnp.max(scores, axis=1, keepdims=True)
+        expo = jnp.exp(scores - top)
+        total = jnp.sum(expo, axis=1, keepdims=True)
+        mixed = jnp.dot(expo.astype(jnp.bfloat16), v_ref[g], preferred_element_type=jnp.float32)
+        out_ref[g] = mixed / total
+        level = jnp.where(lane == new_rows + g, top + jnp.log(total), level)
+    weight_ref[...] = level
+
+
+def attend_cached(queries, key_cache, value_cache, cache_lengths):
+    sequences, new_rows, qheads, head_size = queries.shape
+    _, groups, slots, _ = key_cache.shape
+    rows = new_rows * (qheads // groups)
+    cache_spec = pl.BlockSpec((None, groups, slots, head_size), lambda s, n: (s, 0, 0, 0))
+    return pl.pallas_call(
+        cached_kernel,
+        out_shape=(
+            jax.ShapeDtypeStruct((sequences, groups, rows, head_size), jnp.float32),
+            jax.ShapeDtypeStruct((sequences, rows, 128), jnp.float32),
+        ),
+        grid_spec=pltpu.PrefetchScalarGridSpec(
+            num_scalar_prefetch=1,
+            grid=(sequences,),
+            in_specs=[
+                pl.BlockSpec((None, new_rows, qheads, head_size), lambda s, n: (s, 0, 0, 0)),
+                cache_spec,
+                cache_spec,
+            ],
+            out_specs=(
+                pl.BlockSpec((None, groups, rows, head_size), lambda s, n: (s, 0, 0, 0)),
+                pl.BlockSpec((None, rows, 128), lambda s, n: (s, 0, 0)),
+            ),
+        ),
+        compiler_params=pltpu.CompilerParams(vmem_limit_bytes=40 * 1024 * 1024),
+        cost_estimate=pl.CostEstimate(
+            flops=4 * sequences * groups * rows * slots * head_size,
+            bytes_accessed=12 * 1024 * 1024,
+            transcendentals=sequences * groups * rows * slots,
+        ),
+        name="attend_cached",
+    )(cache_lengths, queries, key_cache, value_cache)
+
+
+def finish_kernel(
+    lengths, gain_ref, cos_ref, sin_ref, a_ref, b_ref, c_ref, q_ref, cached_ref, weight_ref, entry_ref, out_ref
+):
+    live = lengths[pl.program_id(0)]
+    new_rows, qheads, head_size = q_ref.shape
+    groups = cached_ref.shape[0]
+    share = qheads // groups
+    rows = new_rows * share
+    half = head_size // 2
+    scale = 1.0 / math.sqrt(head_size)
+    projected = a_ref[...] + b_ref[...] + c_ref[...].astype(jnp.float32)
+    gain = gain_ref[...].astype(jnp.float32)
+    cosine, sine = cos_ref[...], sin_ref[...]
+    queries = q_ref[...].astype(jnp.float32)
+    level = weight_ref[...]
+    lane = lax.broadcasted_iota(jnp.int32, (rows, 128), 1)
+    token = lax.broadcasted_iota(jnp.int32, (rows, 128), 0) // share
+    causal = jnp.logical_and(lane <= token, lane < new_rows)
+    shown = token < live
+    padding = jnp.zeros((128 - new_rows, head_size), jnp.bfloat16)
+    results = []
+    for g in range(groups):
+        raw = projected[:, g * head_size : (g + 1) * head_size]
+        normed = raw / jnp.sqrt(jnp.mean(raw * raw, axis=1, keepdims=True) + 1e-06) * gain
+        swapped = jnp.concatenate([normed[:, half:], normed[:, :half]], axis=1)
+        key = (normed * cosine + swapped * sine).astype(jnp.bfloat16)
+        value = projected[:, (groups + g) * head_size : (groups + g + 1) * head_size].astype(jnp.bfloat16)
+        entry_ref[:, 0, g * head_size : (g + 1) * head_size] = key
+        entry_ref[:, 1, g * head_size : (g + 1) * head_size] = value
+        asked = queries[:, g * share : (g + 1) * share, :].reshape(rows, head_size).astype(jnp.bfloat16)
+        scores = lax.dot_general(
+            asked,
+            jnp.concatenate([key, padding], axis=0),
+            (((1,), (1,)), ((), ())),
+            preferred_element_type=jnp.float32,
+        )
+        kept = jnp.where(lane == new_rows + g, level, MASKED)
+        scores = jnp.where(causal, scores * scale, kept)
+        expo = jnp.exp(scores - jnp.max(scores, axis=1, keepdims=True))
+        total = jnp.sum(expo, axis=1, keepdims=True)
+        mixed = jnp.dot(
+            expo.astype(jnp.bfloat16), jnp.concatenate([value, padding], axis=0), preferred_element_type=jnp.float32
+        )
+        mixed = (mixed + expo[:, new_rows + g : new_rows + g + 1] * cached_ref[g]) / total
+        results.append(jnp.where(shown, mixed, 0.0).reshape(new_rows, share, head_size))
+    out_ref[...] = jnp.concatenate(results, axis=1).astype(jnp.bfloat16)
+
+
+def finish(tool_lengths, key_gain, cosine, sine, parts, queries, cached, weight):
+    sequences, new_rows, qheads, head_size = queries.shape
+    _, groups, rows, _ = cached.shape
+    width = parts[0].shape[1]
+    row_spec = pl.BlockSpec((new_rows, width), lambda s, n: (s, 0))
+    angle_spec = pl.BlockSpec((new_rows, head_size), lambda s, n: (s, 0))
+    query_spec = pl.BlockSpec((None, new_rows, qheads, head_size), lambda s, n: (s, 0, 0, 0))
+    return pl.pallas_call(
+        finish_kernel,
+        out_shape=(
+            jax.ShapeDtypeStruct((sequences, new_rows, 2, width // 2), jnp.bfloat16),
+            jax.ShapeDtypeStruct(queries.shape, jnp.bfloat16),
+        ),
+        grid_spec=pltpu.PrefetchScalarGridSpec(
+            num_scalar_prefetch=1,
+            grid=(sequences,),
+            in_specs=[
+                pl.BlockSpec((1, head_size), lambda s, n: (0, 0)),
+                angle_spec,
+                angle_spec,
+                row_spec,
+                row_spec,
+                row_spec,
+                query_spec,
+                pl.BlockSpec((None, groups, rows, head_size), lambda s, n: (s, 0, 0, 0)),
+                pl.BlockSpec((None, rows, 128), lambda s, n: (s, 0, 0)),
+            ],
+            out_specs=(
+                pl.BlockSpec((None, new_rows, 2, width // 2), lambda s, n: (s, 0, 0, 0)),
+                query_spec,
+            ),
+        ),
+        compiler_params=pltpu.CompilerParams(vmem_limit_bytes=40 * 1024 * 1024),
+        name="finish",
+    )(tool_lengths, key_gain.reshape(1, head_size), cosine, sine, *parts, queries, cached, weight)
+
+
+def fast_device(
+    master,
+    gradient,
+    first_moment,
+    second_moment,
+    key_gain,
+    hidden,
+    queries,
+    key_cache,
+    value_cache,
+    cache_lengths,
+    tool_lengths,
+):
+    sequences, new_rows, model_width = hidden.shape
+    groups, head_size = key_cache.shape[1], key_cache.shape[3]
+    count = sequences * new_rows
+    tokens = hidden.reshape(count, model_width)
+    role = lax.axis_index("role")
+    depth = model_width // lax.axis_size("role")
+
+    def block(index):
+        return lax.dynamic_slice_in_dim(tokens, index * depth, depth, 1)
+
+    blocks = [
+        block(role),
+        lax.ppermute(block(role ^ 1), "role", CORE_SWAP),
+        lax.ppermute(block(role ^ 2), "role", X_SWAP),
+        lax.ppermute(block(role ^ 3), "role", DIAGONAL),
+    ]
+    updated, moment_one, moment_two, own, other = adam_step(
+        master, gradient, first_moment, second_moment, groups
+    )
+    swapped = lax.ppermute(other, "tp", TP_SWAP)
+    units = [own, swapped]
+    far = [lax.ppermute(unit, "fsdp", Z_FAR) for unit in units]
+    near = [lax.ppermute(unit, "fsdp", Z_NEAR) for unit in units]
+    ends = [lax.ppermute(unit, "fsdp", Z_ENDS) for unit in far]
+    middle = [lax.ppermute(unit, "fsdp", Z_MIDDLE) for unit in units]
+    keep, send = project(blocks, units + near + far + middle + ends)
+    crossed = lax.ppermute(send, "role", CORE_SWAP)
+    outgoing = (keep[1] + crossed[1]).astype(jnp.bfloat16)
+    arrived = lax.ppermute(outgoing, "role", X_SWAP)
+
+    positions = (cache_lengths[:, None] + jnp.arange(new_rows, dtype=jnp.int32)[None, :]).reshape(count)
+    half = head_size // 2
+    inverse = rope_theta ** (-(jnp.arange(half, dtype=jnp.float32) * 2.0) / head_size)
+    angles = positions.astype(jnp.float32)[:, None] * inverse[None, :]
+    cosine, sine = jnp.cos(angles), jnp.sin(angles)
+    cosine = jnp.concatenate([cosine, cosine], axis=1)
+    sine = jnp.concatenate([-sine, sine], axis=1)
+    cached, weight = attend_cached(queries, key_cache, value_cache, cache_lengths)
+    new_entries, attended = finish(
+        tool_lengths,
+        key_gain,
+        cosine,
+        sine,
+        (keep[0], crossed[0], arrived),
+        queries,
+        cached,
+        weight,
+    )
+    return (updated, moment_one, moment_two, new_entries, attended)
+
+
+def device_program(mesh):
+    sizes = (mesh.shape["role"], mesh.shape["fsdp"], mesh.shape["tp"])
+    return fast_device if sizes == (4, 4, 2) else plain_device
+
+
 def solution(mesh):
     return jax.shard_map(
-        per_device,
+        device_program(mesh),
         mesh=mesh,
         in_specs=(
             P(("role", "fsdp", "tp"), None, None),

time: 188 us -> 101 us (0.54)
  waiting for transfers between devices: 89.2 us -> 40.3 us
  local copies, waits for them, and re-layouts: 48.9 us -> 3.69 us
  starting transfers between devices: 0.08 us -> 28.6 us
  Pallas kernels: 0 us -> 25.5 us
  matrix products: 19.8 us -> 0 us
  between operations: 14.3 us -> 0.79 us
  other arithmetic: 14.2 us -> 2.35 us
    all_gather x1 -> x0, waiting for transfers between devices: 70.8 us -> none  [per_device(): tp_rows = lax.all_gather(weights, ('role', 'fsdp'), axis=0, tiled=True)]
    ppermute x0 -> x14, waiting for transfers between devices: none -> 40.3 us  [the longest x2 19.7 us: fast_device(): ends = [lax.ppermute(unit, 'fsdp', Z_ENDS) for unit in far]]
    ppermute x0 -> x14, starting transfers between devices: none -> 28.6 us  [the longest x2 15.7 us: fast_device(): near = [lax.ppermute(unit, 'fsdp', Z_NEAR) for unit in units]]
    reshape x2 -> x0, local copies, waits for them, and re-layouts: 27.6 us -> none  [the longest x1 26.2 us: per_device(): tp_rows.reshape(tp_rows.shape[0], -1)]
    pallas_call x0 -> x4, Pallas kernels: none -> 25.5 us  [the longest x1 10.5 us: finish(): pl.pallas_call(finish_kernel, out_shape=(jax.ShapeDtypeStruct((sequences,...]
    dot_general x5 -> x0, matrix products: 19.8 us -> none  [the longest x1 8.81 us: per_device(): jnp.dot(picked, tp_rows.reshape(tp_rows.shape[0], -1), preferred_element_...]
    reduce_scatter x1 -> x0, waiting for transfers between devices: 18.4 us -> none  [per_device(): lax.psum_scatter(partial_value.reshape(row_count, 2, weights.shape[2]), '...]
    dynamic_slice x2 -> x1, local copies, waits for them, and re-layouts: 15.2 us -> 0.19 us  [block(): return lax.dynamic_slice_in_dim(tokens, index * depth, depth, 1)]
  transfers between devices with their start and end apart: 2 -> 14, of which waited for: 2 -> 7; matrix products, arithmetic and copies ran while one was open for 14% -> 1% of each run, Pallas kernels for 0% -> 5%
where the time goes in v1:
time: 101 us
  waiting for transfers between devices  40.3 us (40%)
  starting transfers between devices  28.6 us (28%)
  Pallas kernels  25.5 us (25%)
  local copies, waits for them, and re-layouts  3.69 us (4%)
  other arithmetic  2.35 us (2%)
    ppermute x2, waiting for transfers between devices, fast_device(): ends = [lax.ppermute(unit, 'fsdp', Z_ENDS) for unit in far]  19.7 us
    ppermute x2, starting transfers between devices, fast_device(): near = [lax.ppermute(unit, 'fsdp', Z_NEAR) for unit in units]  15.7 us
    pallas_call x1, Pallas kernels, finish(): pl.pallas_call(finish_kernel, out_shape=(jax.ShapeDtypeStruct((sequences,...  10.5 us
    ppermute x2, waiting for transfers between devices, fast_device(): far = [lax.ppermute(unit, 'fsdp', Z_FAR) for unit in units]  7.21 us
    pallas_call x1, Pallas kernels, adam_step(): pl.pallas_call(functools.partial(adam_kernel, head_count), out_shape=(fla...  7.04 us
    ppermute x1, waiting for transfers between devices, fast_device(): swapped = lax.ppermute(other, 'tp', TP_SWAP)  5.75 us
    pallas_call x1, Pallas kernels, attend_cached(): pl.pallas_call(cached_kernel, out_shape=(jax.ShapeDtypeStruct((sequences,...  4.76 us
    ppermute x1, waiting for transfers between devices, fast_device(): arrived = lax.ppermute(outgoing, 'role', X_SWAP)  4.28 us
  transfers between devices with their start and end apart: 14, of which 7 were waited for; matrix products, arithmetic and copies ran while one was open for 1% of the time, Pallas kernels for 5%

profile of v1, /device:TPU:0, one launch (start us, length us, event | category | flops | bytes accessed | tf_op | source)
XLA Modules:
  0.0 101.1 jit_solution(5974517179162901866)
XLA Ops:
  0.6 7.0 %adam.1 = (f32[2560,128]{1,0:T(8,128)}, f32[2560,128]{1,0:T(8,128)}, f32[2560,128]{1,0:T(8,128)}, bf16[160,1024]{1,0:T(8,128)(2,1)}, bf16[160,1024]{1,0:T(8,128)(2,1)}) custom-call(f32[2560,128]{1,0:T(8,128)} %bitcast.45, f32[2560,128]{1,0:T(8,128)} %bitcast.46, f32[2560,128]{1,0:T(8,128)} %bitcast.47, f32[2560,128]{1,0:T(8,128)} %bitcast.48), custom_call_target="tpu_custom_call" | custom-call | flops 6553600 | bytes 10485760 | tf_op jit(solution)/shard_map/adam/pallas_call | solution.py:188
  7.7 4.1 %collective-permute-start.6 = (bf16[160,1024]{1,0:T(8,128)(2,1)}, bf16[160,1024]{1,0:T(8,128)(2,1)S(1)}, u32[]{:S(2)}, u32[]{:S(2)}) collective-permute-start(bf16[160,1024]{1,0:T(8,128)(2,1)} %get-tuple-element.19.o0), channel_id=1, source_target_pairs={{0,4},{4,0},{2,6},{6,2},{1,5},{5,1},{3,7},{7,3},{8,12},{12,8},{10,... | collective-permute-start | bytes 983048 | tf_op jit(solution)/shard_map/ppermute | solution.py:443
  11.8 1.6 %collective-permute-start.4 = (bf16[160,1024]{1,0:T(8,128)(2,1)}, bf16[160,1024]{1,0:T(8,128)(2,1)S(1)}, u32[]{:S(2)}, u32[]{:S(2)}) collective-permute-start(bf16[160,1024]{1,0:T(8,128)(2,1)} %get-tuple-element.19.o0), channel_id=1, source_target_pairs={{0,2},{2,0},{4,6},{6,4},{1,3},{3,1},{5,7},{7,5},{8,10},{10,8},{12,... | collective-permute-start | bytes 983048 | tf_op jit(solution)/shard_map/ppermute | solution.py:444
  13.3 1.5 %collective-permute-start.3 = (bf16[160,1024]{1,0:T(8,128)(2,1)}, bf16[160,1024]{1,0:T(8,128)(2,1)S(1)}, u32[]{:S(2)}, u32[]{:S(2)}) collective-permute-start(bf16[160,1024]{1,0:T(8,128)(2,1)} %get-tuple-element.20), channel_id=1, source_target_pairs={{0,1},{1,0},{2,3},{3,2},{4,5},{5,4},{6,7},{7,6},{8,9},{9,8},{10,11... | collective-permute-start | bytes 983048 | tf_op jit(solution)/shard_map/ppermute | solution.py:441
  15.1 1.6 %collective-permute-start.1 = (bf16[192,1280]{1,0:T(8,128)(2,1)S(1)}, bf16[192,1280]{1,0:T(8,128)(2,1)S(1)}, u32[]{:S(2)}, u32[]{:S(2)}) collective-permute-start(bf16[192,1280]{1,0:T(8,128)(2,1)S(1)} %get-tuple-element.28), channel_id=1, source_target_pairs={{0,16},{8,24},{16,0},{24,8},{1,17},{9,25},{17,1},{25,9},{2,18},{10... | collective-permute-start | bytes 1474568 | tf_op jit(solution)/shard_map/ppermute | solution.py:435
  16.7 5.7 %collective-permute-done.3.p0 = bf16[160,1024]{1,0:T(8,128)(2,1)S(1)} collective-permute-done((bf16[160,1024]{1,0:T(8,128)(2,1)}, bf16[160,1024]{1,0:T(8,128)(2,1)S(1)}, u32[]{:S(2)}, u32[]{:S(2)}) %collective-permute-start.3) | collective-permute-done | bytes 327712 | tf_op jit(solution)/shard_map/ppermute | solution.py:441
  23.1 4.5 %collective-permute-done.6.o2 = bf16[160,1024]{1,0:T(8,128)(2,1)S(1)} collective-permute-done((bf16[160,1024]{1,0:T(8,128)(2,1)}, bf16[160,1024]{1,0:T(8,128)(2,1)S(1)}, u32[]{:S(2)}, u32[]{:S(2)}) %collective-permute-start.6) | collective-permute-done | bytes 327712 | tf_op jit(solution)/shard_map/ppermute | solution.py:443
  27.6 0.7 copy-done.7
  28.3 14.1 %collective-permute-start.5 = (bf16[160,1024]{1,0:T(8,128)(2,1)S(1)}, bf16[160,1024]{1,0:T(8,128)(2,1)S(1)}, u32[]{:S(2)}, u32[]{:S(2)}) collective-permute-start(bf16[160,1024]{1,0:T(8,128)(2,1)S(1)} %collective-permute-done.3.p0), channel_id=1, source_target_pairs={{0,2},{2,0},{4,6},{6,4},{1,3},{3,1},{5,7},{7,5},{8,10},{10,8},{12,... | collective-permute-start | bytes 983048 | tf_op jit(solution)/shard_map/ppermute | solution.py:444
  42.5 1.3 %collective-permute-start.10 = (bf16[160,1024]{1,0:T(8,128)(2,1)S(1)}, bf16[160,1024]{1,0:T(8,128)(2,1)S(1)}, u32[]{:S(2)}, u32[]{:S(2)}) collective-permute-start(bf16[160,1024]{1,0:T(8,128)(2,1)S(1)} %collective-permute-done.6.o2), channel_id=1, source_target_pairs={{4,6},{2,0},{5,7},{3,1},{12,14},{10,8},{13,15},{11,9},{20,22},{18,... | collective-permute-start | bytes 983048 | tf_op jit(solution)/shard_map/ppermute | solution.py:445
  44.5 0.7 copy-done.9
  45.2 2.8 %collective-permute-done.7.p2 = bf16[160,1024]{1,0:T(8,128)(2,1)S(1)} collective-permute-done((bf16[160,1024]{1,0:T(8,128)(2,1)S(1)}, bf16[160,1024]{1,0:T(8,128)(2,1)S(1)}, u32[]{:S(2)}, u32[]{:S(2)}) %collective-permute-start.7) | collective-permute-done | bytes 327712 | tf_op jit(solution)/shard_map/ppermute | solution.py:443
  47.9 1.3 %collective-permute-start.11 = (bf16[160,1024]{1,0:T(8,128)(2,1)S(1)}, bf16[160,1024]{1,0:T(8,128)(2,1)S(1)}, u32[]{:S(2)}, u32[]{:S(2)}) collective-permute-start(bf16[160,1024]{1,0:T(8,128)(2,1)S(1)} %collective-permute-done.7.p2), channel_id=1, source_target_pairs={{4,6},{2,0},{5,7},{3,1},{12,14},{10,8},{13,15},{11,9},{20,22},{18,... | collective-permute-start | bytes 983048 | tf_op jit(solution)/shard_map/ppermute | solution.py:445
  49.2 12.7 %collective-permute-done.10.oe = bf16[160,1024]{1,0:T(8,128)(2,1)S(1)} collective-permute-done((bf16[160,1024]{1,0:T(8,128)(2,1)S(1)}, bf16[160,1024]{1,0:T(8,128)(2,1)S(1)}, u32[]{:S(2)}, u32[]{:S(2)}) %collective-permute-start.10) | collective-permute-done | bytes 327712 | tf_op jit(solution)/shard_map/ppermute | solution.py:445
  62.0 6.9 %collective-permute-done.11.pe = bf16[160,1024]{1,0:T(8,128)(2,1)S(1)} collective-permute-done((bf16[160,1024]{1,0:T(8,128)(2,1)S(1)}, bf16[160,1024]{1,0:T(8,128)(2,1)S(1)}, u32[]{:S(2)}, u32[]{:S(2)}) %collective-permute-start.11) | collective-permute-done | bytes 327712 | tf_op jit(solution)/shard_map/ppermute | solution.py:445
  68.9 1.0 copy-done.8
  69.9 1.0 copy-done.10
  70.8 3.2 %project.1 = (f32[2,192,1024]{2,1,0:T(8,128)S(1)}, f32[2,192,1024]{2,1,0:T(8,128)S(1)}) custom-call(bf16[192,1280]{1,0:T(8,128)(2,1)S(1)} %get-tuple-element.30.h0, bf16[192,1280]{1,0:T(8,128)(2,1)S(1)} %collective-permute-done.h1, bf16[192,1280]{1,0:T(8,128)(2,1)S(1)} %collective-permute-done.1.h2, bf16[192,1280]{1,0:T(8,128)(2,1)S(1)} %collective-permute-done.2.h3, ...), custom_call_target="tpu_custom_call" | custom-call | flops 2013265920 | bytes 5767168 | tf_op jit(solution)/shard_map/project/pallas_call | solution.py:250
  74.3 3.3 %collective-permute-done.12 = f32[2,192,1024]{2,1,0:T(8,128)} collective-permute-done((f32[2,192,1024]{2,1,0:T(8,128)S(1)}, f32[2,192,1024]{2,1,0:T(8,128)}, u32[]{:S(2)}, u32[]{:S(2)}) %collective-permute-start.12) | collective-permute-done | bytes 1572896 | tf_op jit(solution)/shard_map/ppermute | solution.py:448
  77.6 1.7 %fusion.1 = (bf16[192,1024]{1,0:T(8,128)(2,1)S(1)}, f32[192,1024]{1,0:T(8,128)S(1)}, f32[192,1024]{1,0:T(8,128)S(1)}) fusion(f32[2,192,1024]{2,1,0:T(8,128)} %collective-permute-done.12, f32[2,192,1024]{2,1,0:T(8,128)S(1)} %get-tuple-element.21), kind=kLoop, calls=%fused_computation.4 | loop fusion | flops 393216 | bytes 5111808 | tf_op jit(solution)/shard_map/convert_element_type | solution.py:449
  79.4 1.6 %collective-permute-start.13 = (bf16[192,1024]{1,0:T(8,128)(2,1)S(1)}, bf16[192,1024]{1,0:T(8,128)(2,1)S(1)}, u32[]{:S(2)}, u32[]{:S(2)}) collective-permute-start(bf16[192,1024]{1,0:T(8,128)(2,1)S(1)} %get-tuple-element.31), channel_id=1, source_target_pairs={{0,16},{8,24},{16,0},{24,8},{1,17},{9,25},{17,1},{25,9},{2,18},{10... | collective-permute-start | bytes 1179656 | tf_op jit(solution)/shard_map/ppermute | solution.py:450
  81.0 4.8 %attend_cached.1 = (f32[4,4,384,128]{3,2,1,0:T(8,128)S(1)}, f32[4,384,128]{2,1,0:T(8,128)S(1)}) custom-call(s32[4]{0:T(128)S(1)} %copy-done.3, bf16[4,48,32,128]{3,2,1,0:T(8,128)(2,1)S(1)} %copy-done, bf16[4,4,192,128]{3,2,1,0:T(8,128)(2,1)S(1)} %copy-done.1, bf16[4,4,192,128]{3,2,1,0:T(8,128)(2,1)S(1)} %copy-done.2), custom_call_target="tpu_custom_call" | custom-call | flops 603979776 | bytes 12582912 | tf_op jit(solution)/shard_map/attend_cached/pallas_call | solution.py:295
  86.3 4.3 %collective-permute-done.13.c_ref = bf16[192,1024]{1,0:T(8,128)(2,1)S(1)} collective-permute-done((bf16[192,1024]{1,0:T(8,128)(2,1)S(1)}, bf16[192,1024]{1,0:T(8,128)(2,1)S(1)}, u32[]{:S(2)}, u32[]{:S(2)}) %collective-permute-start.13) | collective-permute-done | bytes 393248 | tf_op jit(solution)/shard_map/ppermute | solution.py:450
  90.6 10.5 %finish.1 = (bf16[4,48,2,512]{3,2,1,0:T(2,128)(2,1)}, bf16[4,48,32,128]{3,2,1,0:T(8,128)(2,1)}) custom-call(s32[4]{0:T(128)S(1)} %copy-done.4, bf16[1,128]{1,0:T(2,128)(2,1)S(1)} %bitcast.43, f32[192,128]{1,0:T(8,128)S(1)} %get-tuple-element.37.cos_ref, f32[192,128]{1,0:T(8,128)S(1)} %get-tuple-element.38.sin_ref, f32[192,1024]{1,0:T(8,128)S(1)} %get-tuple-element.32.a_ref, ...), custom_call_target="tpu_custom_call" | custom-call | tf_op jit(solution)/shard_map/finish/pallas_call | solution.py:379
  (39 shorter events, 2.5 us)
Async XLA Ops:
  0.6 14.2 %copy-start.11 = (bf16[4,48,5120]{2,1,0:T(8,128)(2,1)S(1)}, bf16[4,48,5120]{2,1,0:T(8,128)(2,1)}, u32[]{:S(2)}) copy-start(bf16[4,48,5120]{2,1,0:T(8,128)(2,1)} %param.16) | copy-start | bytes 5898244
  7.7 19.9 %collective-permute-start.6 = (bf16[160,1024]{1,0:T(8,128)(2,1)}, bf16[160,1024]{1,0:T(8,128)(2,1)S(1)}, u32[]{:S(2)}, u32[]{:S(2)}) collective-permute-start(bf16[160,1024]{1,0:T(8,128)(2,1)} %get-tuple-element.19.o0), channel_id=1, source_target_pairs={{0,4},{4,0},{2,6},{6,2},{1,5},{5,1},{3,7},{7,3},{8,12},{12,8},{10,... | collective-permute-start | bytes 983048 | tf_op jit(solution)/shard_map/ppermute | solution.py:443
  11.8 15.8 %collective-permute-start.4 = (bf16[160,1024]{1,0:T(8,128)(2,1)}, bf16[160,1024]{1,0:T(8,128)(2,1)S(1)}, u32[]{:S(2)}, u32[]{:S(2)}) collective-permute-start(bf16[160,1024]{1,0:T(8,128)(2,1)} %get-tuple-element.19.o0), channel_id=1, source_target_pairs={{0,2},{2,0},{4,6},{6,4},{1,3},{3,1},{5,7},{7,5},{8,10},{10,8},{12,... | collective-permute-start | bytes 983048 | tf_op jit(solution)/shard_map/ppermute | solution.py:444
  13.3 9.1 %collective-permute-start.3 = (bf16[160,1024]{1,0:T(8,128)(2,1)}, bf16[160,1024]{1,0:T(8,128)(2,1)S(1)}, u32[]{:S(2)}, u32[]{:S(2)}) collective-permute-start(bf16[160,1024]{1,0:T(8,128)(2,1)} %get-tuple-element.20), channel_id=1, source_target_pairs={{0,1},{1,0},{2,3},{3,2},{4,5},{5,4},{6,7},{7,6},{8,9},{9,8},{10,11... | collective-permute-start | bytes 983048 | tf_op jit(solution)/shard_map/ppermute | solution.py:441
  14.9 7.6 %copy-start.6 = (bf16[160,1024]{1,0:T(8,128)(2,1)S(1)}, bf16[160,1024]{1,0:T(8,128)(2,1)}, u32[]{:S(2)}) copy-start(bf16[160,1024]{1,0:T(8,128)(2,1)} %get-tuple-element.19.o0) | copy-start | bytes 983044
  15.1 27.4 %collective-permute-start = (bf16[192,1280]{1,0:T(8,128)(2,1)S(1)}, bf16[192,1280]{1,0:T(8,128)(2,1)S(1)}, u32[]{:S(2)}, u32[]{:S(2)}) collective-permute-start(bf16[192,1280]{1,0:T(8,128)(2,1)S(1)} %get-tuple-element.29), channel_id=1, source_target_pairs={{0,8},{8,0},{16,24},{24,16},{1,9},{9,1},{17,25},{25,17},{2,10},{10... | collective-permute-start | bytes 1474568 | tf_op jit(solution)/shard_map/ppermute | solution.py:434
  15.1 28.6 %collective-permute-start.1 = (bf16[192,1280]{1,0:T(8,128)(2,1)S(1)}, bf16[192,1280]{1,0:T(8,128)(2,1)S(1)}, u32[]{:S(2)}, u32[]{:S(2)}) collective-permute-start(bf16[192,1280]{1,0:T(8,128)(2,1)S(1)} %get-tuple-element.28), channel_id=1, source_target_pairs={{0,16},{8,24},{16,0},{24,8},{1,17},{9,25},{17,1},{25,9},{2,18},{10... | collective-permute-start | bytes 1474568 | tf_op jit(solution)/shard_map/ppermute | solution.py:435
  22.5 5.9 %collective-permute-start.8 = (bf16[160,1024]{1,0:T(8,128)(2,1)S(1)}, bf16[160,1024]{1,0:T(8,128)(2,1)S(1)}, u32[]{:S(2)}, u32[]{:S(2)}) collective-permute-start(bf16[160,1024]{1,0:T(8,128)(2,1)S(1)} %copy-done.6), channel_id=1, source_target_pairs={{2,4},{4,2},{3,5},{5,3},{10,12},{12,10},{11,13},{13,11},{18,20},{2... | collective-permute-start | bytes 983048 | tf_op jit(solution)/shard_map/ppermute | solution.py:446
  27.6 20.3 %collective-permute-start.7 = (bf16[160,1024]{1,0:T(8,128)(2,1)S(1)}, bf16[160,1024]{1,0:T(8,128)(2,1)S(1)}, u32[]{:S(2)}, u32[]{:S(2)}) collective-permute-start(bf16[160,1024]{1,0:T(8,128)(2,1)S(1)} %collective-permute-done.3.p0), channel_id=1, source_target_pairs={{0,4},{4,0},{2,6},{6,2},{1,5},{5,1},{3,7},{7,3},{8,12},{12,8},{10,... | collective-permute-start | bytes 983048 | tf_op jit(solution)/shard_map/ppermute | solution.py:443
  28.3 20.9 %collective-permute-start.2 = (bf16[192,1280]{1,0:T(8,128)(2,1)S(1)}, bf16[192,1280]{1,0:T(8,128)(2,1)S(1)}, u32[]{:S(2)}, u32[]{:S(2)}) collective-permute-start(bf16[192,1280]{1,0:T(8,128)(2,1)S(1)} %get-tuple-element.27), channel_id=1, source_target_pairs={{0,24},{8,16},{16,8},{24,0},{1,25},{9,17},{17,9},{25,1},{2,26},{10... | collective-permute-start | bytes 1474568 | tf_op jit(solution)/shard_map/ppermute | solution.py:436
  28.3 33.6 %collective-permute-start.5 = (bf16[160,1024]{1,0:T(8,128)(2,1)S(1)}, bf16[160,1024]{1,0:T(8,128)(2,1)S(1)}, u32[]{:S(2)}, u32[]{:S(2)}) collective-permute-start(bf16[160,1024]{1,0:T(8,128)(2,1)S(1)} %collective-permute-done.3.p0), channel_id=1, source_target_pairs={{0,2},{2,0},{4,6},{6,4},{1,3},{3,1},{5,7},{7,5},{8,10},{10,8},{12,... | collective-permute-start | bytes 983048 | tf_op jit(solution)/shard_map/ppermute | solution.py:444
  42.5 19.5 %collective-permute-start.10 = (bf16[160,1024]{1,0:T(8,128)(2,1)S(1)}, bf16[160,1024]{1,0:T(8,128)(2,1)S(1)}, u32[]{:S(2)}, u32[]{:S(2)}) collective-permute-start(bf16[160,1024]{1,0:T(8,128)(2,1)S(1)} %collective-permute-done.6.o2), channel_id=1, source_target_pairs={{4,6},{2,0},{5,7},{3,1},{12,14},{10,8},{13,15},{11,9},{20,22},{18,... | collective-permute-start | bytes 983048 | tf_op jit(solution)/shard_map/ppermute | solution.py:445
  43.8 18.2 %collective-permute-start.9 = (bf16[160,1024]{1,0:T(8,128)(2,1)S(1)}, bf16[160,1024]{1,0:T(8,128)(2,1)S(1)}, u32[]{:S(2)}, u32[]{:S(2)}) collective-permute-start(bf16[160,1024]{1,0:T(8,128)(2,1)S(1)} %collective-permute-done.3.p0), channel_id=1, source_target_pairs={{2,4},{4,2},{3,5},{5,3},{10,12},{12,10},{11,13},{13,11},{18,20},{2... | collective-permute-start | bytes 983048 | tf_op jit(solution)/shard_map/ppermute | solution.py:446
  47.9 21.0 %collective-permute-start.11 = (bf16[160,1024]{1,0:T(8,128)(2,1)S(1)}, bf16[160,1024]{1,0:T(8,128)(2,1)S(1)}, u32[]{:S(2)}, u32[]{:S(2)}) collective-permute-start(bf16[160,1024]{1,0:T(8,128)(2,1)S(1)} %collective-permute-done.7.p2), channel_id=1, source_target_pairs={{4,6},{2,0},{5,7},{3,1},{12,14},{10,8},{13,15},{11,9},{20,22},{18,... | collective-permute-start | bytes 983048 | tf_op jit(solution)/shard_map/ppermute | solution.py:445
  68.9 1.0 copy-start.8
  69.9 1.0 copy-start.10
  70.8 3.3 %copy-start.3 = (s32[4]{0:T(128)S(1)}, s32[4]{0:T(128)}, u32[]{:S(2)}) copy-start(s32[4]{0:T(128)} %lengths.2) | copy-start | bytes 52
  74.0 3.6 %collective-permute-start.12 = (f32[2,192,1024]{2,1,0:T(8,128)S(1)}, f32[2,192,1024]{2,1,0:T(8,128)}, u32[]{:S(2)}, u32[]{:S(2)}) collective-permute-start(f32[2,192,1024]{2,1,0:T(8,128)S(1)} %get-tuple-element.22), channel_id=1, source_target_pairs={{0,8},{8,0},{16,24},{24,16},{1,9},{9,1},{17,25},{25,17},{2,10},{10... | collective-permute-start | bytes 4718600 | tf_op jit(solution)/shard_map/ppermute | solution.py:448
  77.6 3.4 %copy-start = (bf16[4,48,32,128]{3,2,1,0:T(8,128)(2,1)S(1)}, bf16[4,48,32,128]{3,2,1,0:T(8,128)(2,1)}, u32[]{:S(2)}) copy-start(bf16[4,48,32,128]{3,2,1,0:T(8,128)(2,1)} %q_ref.3) | copy-start | bytes 4718596
  77.6 3.4 %copy-start.1 = (bf16[4,4,192,128]{3,2,1,0:T(8,128)(2,1)S(1)}, bf16[4,4,192,128]{3,2,1,0:T(8,128)(2,1)}, u32[]{:S(2)}) copy-start(bf16[4,4,192,128]{3,2,1,0:T(8,128)(2,1)} %k_ref.1) | copy-start | bytes 2359300
  77.6 3.4 %copy-start.2 = (bf16[4,4,192,128]{3,2,1,0:T(8,128)(2,1)S(1)}, bf16[4,4,192,128]{3,2,1,0:T(8,128)(2,1)}, u32[]{:S(2)}) copy-start(bf16[4,4,192,128]{3,2,1,0:T(8,128)(2,1)} %v_ref.1) | copy-start | bytes 2359300
  79.4 11.2 %copy-start.4 = (s32[4]{0:T(128)S(1)}, s32[4]{0:T(128)}, u32[]{:S(2)}) copy-start(s32[4]{0:T(128)} %lengths.3) | copy-start | bytes 52
  79.4 11.2 %copy-start.5 = (bf16[128]{0:T(256)(128)(2,1)S(1)}, bf16[128]{0:T(256)(128)(2,1)}, u32[]{:S(2)}) copy-start(bf16[128]{0:T(256)(128)(2,1)} %param.15) | copy-start | bytes 772
  79.4 11.2 %collective-permute-start.13 = (bf16[192,1024]{1,0:T(8,128)(2,1)S(1)}, bf16[192,1024]{1,0:T(8,128)(2,1)S(1)}, u32[]{:S(2)}, u32[]{:S(2)}) collective-permute-start(bf16[192,1024]{1,0:T(8,128)(2,1)S(1)} %get-tuple-element.31), channel_id=1, source_target_pairs={{0,16},{8,24},{16,0},{24,8},{1,17},{9,25},{17,1},{25,9},{2,18},{10... | collective-permute-start | bytes 1179656 | tf_op jit(solution)/shard_map/ppermute | solution.py:450
  (2 other events, 1.5 us)

commit v2 on v0

--- a/solution.py
+++ b/solution.py
@@ -1,8 +1,11 @@
+import functools
 import math
 
 import jax
 import jax.numpy as jnp
 from jax import lax
+from jax.experimental import pallas as pl
+from jax.experimental.pallas import tpu as pltpu
 from jax.sharding import PartitionSpec as P
 
 learn_rate = 0.01
@@ -83,7 +86,7 @@
     return jnp.where(live_rows, result, 0.0).astype(jnp.bfloat16)
 
 
-def per_device(
+def plain_device(
     master,
     gradient,
     first_moment,
@@ -132,9 +135,456 @@
     return (updated, moment_one, moment_two, new_entries, attended)
 
 
+CORE_SWAP = ((0, 1), (1, 0), (2, 3), (3, 2))
+X_SWAP = ((0, 2), (1, 3), (2, 0), (3, 1))
+DIAGONAL = ((0, 3), (1, 2), (2, 1), (3, 0))
+XY_SWAP = tuple((2 * r + t, 2 * (r ^ 2) + 1 - t) for r in range(4) for t in range(2))
+Z_NEAR = ((0, 1), (1, 0), (2, 3), (3, 2))
+Z_FAR = ((0, 2), (2, 0), (1, 3), (3, 1))
+Z_MIDDLE = ((1, 2), (2, 1))
+Z_ENDS = ((2, 3), (1, 0))
+TP_SWAP = ((0, 1), (1, 0))
+MASKED = -1e30
+QUICK = pl.CostEstimate(flops=1, bytes_accessed=1, transcendentals=0)
+VMEM_LIMIT = 60 * 1024 * 1024
+ANY = pl.BlockSpec(memory_space=pl.ANY)
+VMEM = pl.BlockSpec(memory_space=pltpu.VMEM)
+
+
+def hold(value, *others):
+    return lax.optimization_barrier((value, others))[0]
+
+
+def adam_kernel(
+    chunks, m_ref, g_ref, f_ref, s_ref, um_ref, uf_ref, us_ref, q0, q1, q2, q3, m_buf, g_buf, f_buf, s_buf, in_sem, out_sem
+):
+    here = lax.axis_index("tp")
+    x = lax.axis_index("role") // 2
+    size = m_ref.shape[0] // chunks
+    rows = q0.shape[0] // chunks
+    heads = q0.shape[1] // 256
+    ins = ((m_ref, m_buf), (g_ref, g_buf), (f_ref, f_buf), (s_ref, s_buf))
+    outs = ((m_buf, um_ref), (f_buf, uf_ref), (s_buf, us_ref))
+
+    def span(c):
+        return pl.ds(pl.multiple_of(c * size, size), size)
+
+    def load(c, i):
+        return pltpu.make_async_copy(ins[i][0].at[span(c)], ins[i][1].at[span(c)], in_sem.at[c, i])
+
+    def save(c, i):
+        return pltpu.make_async_copy(outs[i][0].at[span(c)], outs[i][1].at[span(c)], out_sem.at[c, i])
+
+    for c in range(chunks):
+        for i in range(4):
+            load(c, i).start()
+
+    def one_chunk(c, _):
+        for i in range(4):
+            load(c, i).wait()
+        base = pl.multiple_of(c * size, size)
+        at = span(c)
+        gradient = g_buf[at]
+        moment_one = 0.9 * f_buf[at] + 0.1 * gradient
+        moment_two = 0.95 * s_buf[at] + 0.05 * gradient * gradient
+        scaled = moment_one * (learn_rate / bias_first)
+        root = jnp.sqrt(moment_two * (1.0 / bias_second)) + 1e-08
+        m_buf[at] = m_buf[at] * (1.0 - learn_rate * decay_rate) - scaled / root
+        f_buf[at] = moment_one
+        s_buf[at] = moment_two
+        target = pl.ds(pl.multiple_of(c * rows, rows), rows)
+        for side, half, out in ((here, x, q0), (here, 1 - x, q1), (1 - here, x, q2), (1 - here, 1 - x, q3)):
+            for kind in range(2):
+                for head in range(heads):
+                    start = base + (2 * heads * side + heads * half + head) * 2 + kind
+                    part = m_buf[pl.ds(start, rows, stride=size // rows), :]
+                    column = (kind * heads + head) * 128
+                    out[target, column : column + 128] = part.astype(jnp.bfloat16)
+        for i in range(3):
+            save(c, i).start()
+        return 0
+
+    lax.fori_loop(0, chunks, one_chunk, 0)
+
+    def drain(c, _):
+        for i in range(3):
+            save(c, i).wait()
+        return 0
+
+    lax.fori_loop(0, chunks, drain, 0)
+
+
+def adam_step(master, gradient, first_moment, second_moment):
+    rows, kinds, width = master.shape
+    blocks = width // 128
+    chunks = 5
+
+    def linear(array):
+        split = array.reshape(rows, kinds, blocks, 128)
+        return split.transpose(0, 2, 1, 3).reshape(rows * kinds * blocks, 128)
+
+    def back(array):
+        return array.reshape(rows, blocks, kinds, 128).transpose(0, 2, 1, 3).reshape(rows, kinds, width)
+
+    flat = jax.ShapeDtypeStruct((rows * kinds * blocks, 128), jnp.float32)
+    quarter = jax.ShapeDtypeStruct((rows, kinds * width // 4), jnp.bfloat16)
+    buffer = pltpu.VMEM(flat.shape, jnp.float32)
+    result = pl.pallas_call(
+        functools.partial(adam_kernel, chunks),
+        out_shape=(flat,) * 3 + (quarter,) * 4,
+        in_specs=[ANY] * 4,
+        out_specs=(ANY,) * 3 + (VMEM,) * 4,
+        scratch_shapes=[buffer] * 4 + [pltpu.SemaphoreType.DMA((chunks, 4)), pltpu.SemaphoreType.DMA((chunks, 3))],
+        compiler_params=pltpu.CompilerParams(vmem_limit_bytes=VMEM_LIMIT),
+        cost_estimate=QUICK,
+        name="adam",
+    )(linear(master), linear(gradient), linear(first_moment), linear(second_moment))
+    return [back(each) for each in result[:3]], result[3:]
+
+
+def cut_kernel(tokens, near_ref, far_ref, core_ref, sems):
+    core = lax.axis_index("role") % 2
+    side = lax.axis_index("tp")
+    depth = near_ref.shape[1]
+    moves = (
+        (2 * side + core, near_ref),
+        (2 * side + 1 - core, far_ref),
+        (1 - core, core_ref.at[0]),
+        (3 - core, core_ref.at[1]),
+    )
+    copies = []
+    for n, (index, out) in enumerate(moves):
+        columns = pl.ds(pl.multiple_of(index * depth, 128), depth)
+        copies.append(pltpu.make_async_copy(tokens.at[:, columns], out, sems.at[n]))
+    for each in copies:
+        each.start()
+    for each in copies:
+        each.wait()
+
+
+def cut(tokens, depth):
+    count = tokens.shape[0]
+    one = jax.ShapeDtypeStruct((count, depth), tokens.dtype)
+    return pl.pallas_call(
+        cut_kernel,
+        out_shape=(one, one, jax.ShapeDtypeStruct((2, count, depth), tokens.dtype)),
+        in_specs=[ANY],
+        out_specs=(VMEM,) * 3,
+        scratch_shapes=[pltpu.SemaphoreType.DMA((4,))],
+        compiler_params=pltpu.CompilerParams(vmem_limit_bytes=6 * 1024 * 1024),
+        cost_estimate=pl.CostEstimate(flops=1, bytes_accessed=8 * 2**20, transcendentals=0),
+        name="cut",
+    )(tokens)
+
+
+def project_kernel(
+    tokens, c, xa, xb, da, db, o0, p0, o1, p1, o2, p2, om, pm, oe, pe, keep_ref, send_ref, held, h_buf, sems
+):
+    z = lax.axis_index("fsdp")
+    x = lax.axis_index("role") // 2
+    core = lax.axis_index("role") % 2
+    t = lax.axis_index("tp")
+    rows = o0.shape[0]
+    depth = xa.shape[1]
+    loads = []
+    for n in range(2):
+        columns = pl.ds(pl.multiple_of((2 * n + core) * depth, 128), depth)
+        loads.append(pltpu.make_async_copy(tokens.at[:, columns], h_buf.at[n], sems.at[n]))
+    for each in loads:
+        each.start()
+
+    def put(value, layer, flip_x, flip_t):
+        start = pl.multiple_of((((x ^ flip_x) * 4 + layer) * 2 + (t ^ flip_t)) * rows, 16)
+        held[pl.ds(start, rows)] = value
+
+    def group(own, others, layer):
+        put(own[...], layer, 0, 0)
+        put(others[0], layer, 1, 0)
+        put(others[1], layer, 0, 1)
+        put(others[2], layer, 1, 1)
+
+    group(o0, p0, z)
+    group(o1, p1, z ^ 1)
+    group(o2, p2, z ^ 2)
+    inner = jnp.logical_or(z == 1, z == 2)
+
+    @pl.when(inner)
+    def _():
+        group(om, pm, z ^ 3)
+
+    @pl.when(jnp.logical_not(inner))
+    def _():
+        group(oe, pe, z ^ 3)
+
+    upper, lower = held[:depth], held[depth:]
+    a_rows = held[pl.ds(pl.multiple_of(t * depth, 16), depth)]
+    b_rows = held[pl.ds(pl.multiple_of((1 - t) * depth, 16), depth)]
+
+    def pair(left, top, right, bottom):
+        return jnp.dot(left, top, preferred_element_type=jnp.float32) + jnp.dot(
+            right, bottom, preferred_element_type=jnp.float32
+        )
+
+    send_ref[0] = pair(c[0], upper, c[1], lower)
+    send_ref[1] = pair(da[...], a_rows, db[...], b_rows)
+    keep_ref[1] = pair(xa[...], a_rows, xb[...], b_rows)
+    for each in loads:
+        each.wait()
+    keep_ref[0] = pair(h_buf[0], upper, h_buf[1], lower)
+
+
+def project(tokens, parts, units):
+    count, depth = parts[1].shape
+    width = units[0].shape[1]
+    result = jax.ShapeDtypeStruct((2, count, width), jnp.float32)
+    return pl.pallas_call(
+        project_kernel,
+        out_shape=(result, result),
+        in_specs=[ANY] + [VMEM] * (len(parts) + len(units)),
+        out_specs=(VMEM, VMEM),
+        scratch_shapes=[
+            pltpu.VMEM((2 * depth, width), jnp.bfloat16),
+            pltpu.VMEM((2, count, depth), jnp.bfloat16),
+            pltpu.SemaphoreType.DMA((2,)),
+        ],
+        compiler_params=pltpu.CompilerParams(vmem_limit_bytes=16 * 1024 * 1024),
+        cost_estimate=QUICK,
+        name="project",
+    )(tokens, *parts, *units)
+
+
+def rotate_kernel(gain_ref, cos_ref, sin_ref, keep_ref, crossed_ref, own_ref, sent_ref):
+    head_size = gain_ref.shape[1]
+    half = head_size // 2
+    heads = own_ref.shape[1] // (2 * head_size)
+    gain = gain_ref[...].astype(jnp.float32)
+    for n, out in ((1, sent_ref), (0, own_ref)):
+        summed = keep_ref[n] + crossed_ref[n]
+        for g in range(heads):
+            raw = summed[:, g * head_size : (g + 1) * head_size]
+            normed = raw / jnp.sqrt(jnp.mean(raw * raw, axis=1, keepdims=True) + 1e-06) * gain
+            swapped = jnp.concatenate([normed[:, half:], normed[:, :half]], axis=1)
+            key = normed * cos_ref[n] + swapped * sin_ref[n]
+            out[:, g * head_size : (g + 1) * head_size] = key.astype(jnp.bfloat16)
+        out[:, heads * head_size :] = summed[:, heads * head_size :].astype(jnp.bfloat16)
+
+
+def rotate(key_gain, cosine, sine, keep, crossed):
+    _, count, width = keep.shape
+    result = jax.ShapeDtypeStruct((count, width), jnp.bfloat16)
+    return pl.pallas_call(
+        rotate_kernel,
+        out_shape=(result, result),
+        in_specs=[VMEM] * 5,
+        out_specs=(VMEM, VMEM),
+        compiler_params=pltpu.CompilerParams(vmem_limit_bytes=8 * 1024 * 1024),
+        cost_estimate=QUICK,
+        name="rotate",
+    )(key_gain.reshape(1, -1), cosine, sine, keep, crossed)
+
+
+def cached_kernel(lengths, q_ref, k_ref, v_ref, out_ref, level_ref):
+    filled = lengths[pl.program_id(0)]
+    groups, slots, head_size = k_ref.shape
+    new_rows, qheads, _ = q_ref.shape
+    share = qheads // groups
+    rows = new_rows * share
+    scale = 1.0 / (math.sqrt(head_size) * math.log(2.0))
+    queries = q_ref[...].astype(jnp.float32)
+    inside = lax.broadcasted_iota(jnp.int32, (rows, slots), 1) < filled
+    lane = lax.broadcasted_iota(jnp.int32, (rows, 128), 1)
+    levels = [jnp.full((rows, 128), MASKED, jnp.float32)] * 2
+    for g in range(groups):
+        pair, place = g // 2, g % 2
+        asked = queries[:, g * share : (g + 1) * share, :].reshape(rows, head_size).astype(jnp.bfloat16)
+        scores = lax.dot_general(
+            asked, k_ref[g], (((1,), (1,)), ((), ())), preferred_element_type=jnp.float32
+        )
+        scores = jnp.where(inside, scores * scale, MASKED)
+        top = jnp.max(scores, axis=1, keepdims=True)
+        expo = jnp.exp2(scores - top)
+        total = jnp.sum(expo, axis=1, keepdims=True)
+        mixed = jnp.dot(expo.astype(jnp.bfloat16), v_ref[g], preferred_element_type=jnp.float32)
+        out_ref[pair, :, place * share : (place + 1) * share, :] = (mixed / total).reshape(new_rows, share, head_size)
+        level = top + jnp.log(total) * (1.0 / math.log(2.0))
+        levels[place] = jnp.where(lane == 2 * new_rows + pair, level, levels[place])
+    for place in range(2):
+        level_ref[:, place * share : (place + 1) * share, :] = levels[place].reshape(new_rows, share, 128)
+
+
+def attend_cached(queries, key_cache, value_cache, cache_lengths):
+    sequences, new_rows, qheads, head_size = queries.shape
+    _, groups, slots, _ = key_cache.shape
+    pairs = groups // 2
+    rows = new_rows * qheads // pairs
+    cache_spec = pl.BlockSpec((None, groups, slots, head_size), lambda s, n: (s, 0, 0, 0))
+    return pl.pallas_call(
+        cached_kernel,
+        out_shape=(
+            jax.ShapeDtypeStruct((sequences, pairs, new_rows, qheads // pairs, head_size), jnp.float32),
+            jax.ShapeDtypeStruct((sequences, new_rows, qheads // pairs, 128), jnp.float32),
+        ),
+        grid_spec=pltpu.PrefetchScalarGridSpec(
+            num_scalar_prefetch=1,
+            grid=(sequences,),
+            in_specs=[
+                pl.BlockSpec((None, new_rows, qheads, head_size), lambda s, n: (s, 0, 0, 0)),
+                cache_spec,
+                cache_spec,
+            ],
+            out_specs=(
+                pl.BlockSpec((None, pairs, new_rows, qheads // pairs, head_size), lambda s, n: (s, 0, 0, 0, 0)),
+                pl.BlockSpec((None, new_rows, qheads // pairs, 128), lambda s, n: (s, 0, 0, 0)),
+            ),
+        ),
+        compiler_params=pltpu.CompilerParams(vmem_limit_bytes=16 * 1024 * 1024),
+        cost_estimate=pl.CostEstimate(flops=4 * 10**9, bytes_accessed=12 * 2**20, transcendentals=10**6),
+        name="attend_cached",
+    )(cache_lengths, queries, key_cache, value_cache)
+
+
+def finish_kernel(lengths, place_ref, kv_ref, q_ref, cached_ref, level_ref, *rest):
+    entry_ref, out_ref = rest[-2:]
+    live = lengths[pl.program_id(0)]
+    which = place_ref[0]
+    new_rows, asked_heads, head_size = q_ref.shape
+    share = asked_heads // 2
+    rows = new_rows * asked_heads
+    scale = 1.0 / (math.sqrt(head_size) * math.log(2.0))
+    lane = lax.broadcasted_iota(jnp.int32, (rows, 128), 1)
+    row = lax.broadcasted_iota(jnp.int32, (rows, 128), 0)
+    token = row // asked_heads
+    offset = lane - new_rows * ((row // share) % 2)
+    causal = jnp.logical_and(offset >= 0, offset <= token)
+    stored = lane == 2 * new_rows + which
+    padding = jnp.zeros((128 - 2 * new_rows, head_size), jnp.bfloat16)
+    entry_ref[:, 0, :] = kv_ref[:, : 2 * head_size]
+    entry_ref[:, 1, :] = kv_ref[:, 2 * head_size :]
+
+    def stacked(first):
+        left = kv_ref[:, first * head_size : (first + 1) * head_size]
+        right = kv_ref[:, (first + 1) * head_size : (first + 2) * head_size]
+        return jnp.concatenate([left, right, padding], axis=0)
+
+    scores = lax.dot_general(
+        q_ref[...].reshape(rows, head_size),
+        stacked(0),
+        (((1,), (1,)), ((), ())),
+        preferred_element_type=jnp.float32,
+    )
+    kept = jnp.where(stored, level_ref[...].reshape(rows, 128), MASKED)
+    scores = jnp.where(causal, scores * scale, kept)
+    expo = jnp.exp2(scores - jnp.max(scores, axis=1, keepdims=True))
+    total = jnp.sum(expo, axis=1, keepdims=True)
+    share_cached = jnp.sum(jnp.where(stored, expo, 0.0), axis=1, keepdims=True)
+    mixed = jnp.dot(expo.astype(jnp.bfloat16), stacked(2), preferred_element_type=jnp.float32)
+    mixed = (mixed + share_cached * cached_ref[...].reshape(rows, head_size)) / total
+    out_ref[...] = jnp.where(token < live, mixed, 0.0).reshape(q_ref.shape).astype(jnp.bfloat16)
+
+
+def finish(tool_lengths, which, kv, queries, cached, level, earlier):
+    sequences, new_rows, qheads, head_size = queries.shape
+    _, pairs, _, _, _ = cached.shape
+    heads = qheads // pairs
+    width = kv.shape[1]
+    query_spec = pl.BlockSpec((None, new_rows, qheads // pairs, head_size), lambda s, n, w: (s, 0, w[0], 0))
+    entry_spec = pl.BlockSpec((None, new_rows, 2, width // 2), lambda s, n, w: (s, 0, 0, w[0]))
+    return pl.pallas_call(
+        finish_kernel,
+        out_shape=(
+            jax.ShapeDtypeStruct((sequences, new_rows, 2, pairs * width // 2), jnp.bfloat16),
+            jax.ShapeDtypeStruct(queries.shape, jnp.bfloat16),
+        ),
+        grid_spec=pltpu.PrefetchScalarGridSpec(
+            num_scalar_prefetch=2,
+            grid=(sequences,),
+            in_specs=[
+                pl.BlockSpec((new_rows, width), lambda s, n, w: (s, 0)),
+                query_spec,
+                pl.BlockSpec((None, None, new_rows, heads, head_size), lambda s, n, w: (s, w[0], 0, 0, 0)),
+                pl.BlockSpec((None, new_rows, heads, 128), lambda s, n, w: (s, 0, 0, 0)),
+            ]
+            + [ANY] * len(earlier),
+            out_specs=(entry_spec, query_spec),
+        ),
+        input_output_aliases={6 + n: n for n in range(len(earlier))},
+        compiler_params=pltpu.CompilerParams(vmem_limit_bytes=12 * 1024 * 1024),
+        cost_estimate=QUICK,
+        name="finish",
+    )(tool_lengths, which.reshape(1), kv, queries, cached, level, *earlier)
+
+
+def fast_device(
+    master,
+    gradient,
+    first_moment,
+    second_moment,
+    key_gain,
+    hidden,
+    queries,
+    key_cache,
+    value_cache,
+    cache_lengths,
+    tool_lengths,
+):
+    sequences, new_rows, model_width = hidden.shape
+    head_size = key_cache.shape[3]
+    count = sequences * new_rows
+    tokens = hidden.reshape(count, model_width)
+    x = lax.axis_index("role") // 2
+    depth = model_width // lax.axis_size("role")
+
+    (updated, moment_one, moment_two), quarters = adam_step(master, gradient, first_moment, second_moment)
+    own = quarters[0]
+    from_x = lax.ppermute(quarters[1], "role", X_SWAP)
+    from_y = lax.ppermute(quarters[2], "tp", TP_SWAP)
+    from_xy = lax.ppermute(quarters[3], ("role", "tp"), XY_SWAP)
+    near_cut, far_cut, core_cut = cut(hold(tokens, own), depth)
+    own = hold(own, near_cut)
+    far_own, near_own, middle_own = (lax.ppermute(own, "fsdp", pairs) for pairs in (Z_FAR, Z_NEAR, Z_MIDDLE))
+    near_x = lax.ppermute(near_cut, "role", X_SWAP)
+    rest = jnp.stack(hold((from_x, from_y, from_xy), far_own, near_own, middle_own))
+    far_rest = lax.ppermute(rest, "fsdp", Z_FAR)
+    near_rest = lax.ppermute(rest, "fsdp", Z_NEAR)
+    far_x = lax.ppermute(hold(far_cut, rest), "role", DIAGONAL)
+    crossed_tokens = lax.ppermute(hold(core_cut, rest), "role", CORE_SWAP)
+    cached, level = attend_cached(queries, key_cache, value_cache, hold(cache_lengths, rest))
+    near_y = lax.ppermute(hold(near_x, level), "tp", TP_SWAP)
+    far_y = lax.ppermute(hold(far_x, level), "tp", TP_SWAP)
+    ends_own = lax.ppermute(hold(far_own, level), "fsdp", Z_ENDS)
+    ready = (far_rest, near_rest, near_y, ends_own)
+    ends_rest = lax.ppermute(hold(far_rest, *ready), "fsdp", Z_ENDS)
+    middle_rest = lax.ppermute(hold(rest, *ready), "fsdp", Z_MIDDLE)
+    lengths_x = lax.ppermute(hold(cache_lengths, *ready), "role", X_SWAP)
+
+    lengths = jnp.stack([cache_lengths, lengths_x])
+    positions = (lengths[:, :, None] + jnp.arange(new_rows, dtype=jnp.int32)[None, None, :]).reshape(2, count)
+    half = head_size // 2
+    inverse = rope_theta ** (-(jnp.arange(half, dtype=jnp.float32) * 2.0) / head_size)
+    angles = positions.astype(jnp.float32)[:, :, None] * inverse[None, None, :]
+    cosine, sine = jnp.cos(angles), jnp.sin(angles)
+    cosine = jnp.concatenate([cosine, cosine], axis=2)
+    sine = jnp.concatenate([-sine, sine], axis=2)
+
+    parts = hold((crossed_tokens, near_x, near_y, far_x, far_y), cosine, sine)
+    units = (own, rest, near_own, near_rest, far_own, far_rest, middle_own, middle_rest, ends_own, ends_rest)
+    keep, send = project(tokens, parts, units)
+    crossed = lax.ppermute(send, "role", CORE_SWAP)
+    own_kv, sent_kv = rotate(key_gain, cosine, sine, keep, crossed)
+    arrived_kv = lax.ppermute(sent_kv, "role", X_SWAP)
+    partial = finish(tool_lengths, x, own_kv, queries, cached, level, ())
+    new_entries, attended = finish(tool_lengths, 1 - x, arrived_kv, queries, cached, level, partial)
+    return (updated, moment_one, moment_two, new_entries, attended)
+
+
+def device_program(mesh):
+    sizes = (mesh.shape["role"], mesh.shape["fsdp"], mesh.shape["tp"])
+    return fast_device if sizes == (4, 4, 2) else plain_device
+
+
 def solution(mesh):
     return jax.shard_map(
-        per_device,
+        device_program(mesh),
         mesh=mesh,
         in_specs=(
             P(("role", "fsdp", "tp"), None, None),

time: 188 us -> 95.8 us (0.51)
  the two profiles are of different devices: /device:TPU:0 before, /device:TPU:17 now
where the time goes in v2:
time: 95.8 us; the launch traced here: 95.5 us
  starting transfers between devices  35.8 us (37%)
  Pallas kernels  25.2 us (26%)
  waiting for transfers between devices  23.5 us (25%)
  local copies, waits for them, and re-layouts  8.26 us (9%)
  other arithmetic  1.81 us (2%)
    unnamed x36, local copies, waits for them, and re-layouts  8.02 us
    pallas_call x2, Pallas kernels, finish(): pl.pallas_call(finish_kernel, out_shape=(jax.ShapeDtypeStruct((sequences,...  7.45 us
    ppermute x1, starting transfers between devices, fast_device(): ends_own = lax.ppermute(hold(far_own, level), 'fsdp', Z_ENDS)  6.68 us
    pallas_call x1, Pallas kernels, adam_step(): pl.pallas_call(functools.partial(adam_kernel, chunks), out_shape=(flat,)...  5.38 us
    pallas_call x1, Pallas kernels, project(): pl.pallas_call(project_kernel, out_shape=(result, result), in_specs=[ANY]...  5.23 us
    ppermute x1, waiting for transfers between devices, fast_device(): far_x = lax.ppermute(hold(far_cut, rest), 'role', DIAGONAL)  5.09 us
    pallas_call x1, Pallas kernels, attend_cached(): pl.pallas_call(cached_kernel, out_shape=(jax.ShapeDtypeStruct((sequences,...  4.82 us
    ppermute x1, starting transfers between devices, fast_device(): ends_rest = lax.ppermute(hold(far_rest, *ready), 'fsdp', Z_ENDS)  4.8 us
  transfers between devices with their start and end apart: 19, of which 9 were waited for; matrix products, arithmetic and copies ran while one was open for 2% of the time, Pallas kernels for 9%

profile of v2, /device:TPU:17, one launch (start us, length us, event | category | flops | bytes accessed | tf_op | source)
XLA Modules:
  0.0 95.5 jit_solution(4724621436184931311)
XLA Ops:
  0.6 5.4 %adam.1 = (f32[2560,128]{1,0:T(8,128)}, f32[2560,128]{1,0:T(8,128)}, f32[2560,128]{1,0:T(8,128)}, bf16[160,512]{1,0:T(8,128)(2,1)}, bf16[160,512]{1,0:T(8,128)(2...) custom-call(f32[2560,128]{1,0:T(8,128)} %bitcast.48, f32[2560,128]{1,0:T(8,128)} %bitcast.49, ...), custom_call_target="tpu_custom_call" | custom-call | flops 1 | bytes 1 | tf_op jit(solution)/shard_map/adam/pallas_call | solution.py:232
  7.4 1.4 %collective-permute-start.4 = (bf16[160,512]{1,0:T(8,128)(2,1)S(1)}, bf16[160,512]{1,0:T(8,128)(2,1)S(1)}, u32[]{:S(2)}, u32[]{:S(2)}) collective-permute-start(bf16[160,512]{1,0:T(8,128)(2,1)S(1)} %copy-done.6), channel_id=1, source_target_pairs={{0,2},{2,0},{4,6},{6,4},{1,3},{3,1},{5,7},{7,5},{8,10},{10,8},{12,... | collective-permute-start | bytes 491528 | tf_op jit(solution)/shard_map/ppermute | solution.py:544
  8.8 3.2 %collective-permute-start.5 = (bf16[160,512]{1,0:T(8,128)(2,1)S(1)}, bf16[160,512]{1,0:T(8,128)(2,1)S(1)}, u32[]{:S(2)}, u32[]{:S(2)}) collective-permute-start(bf16[160,512]{1,0:T(8,128)(2,1)S(1)} %copy-done.6), channel_id=1, source_target_pairs={{2,4},{4,2},{3,5},{5,3},{10,12},{12,10},{11,13},{13,11},{18,20},{2... | collective-permute-start | bytes 491528 | tf_op jit(solution)/shard_map/ppermute | solution.py:544
  17.9 3.6 %collective-permute-done.5.om = bf16[160,512]{1,0:T(8,128)(2,1)S(1)} collective-permute-done((bf16[160,512]{1,0:T(8,128)(2,1)S(1)}, bf16[160,512]{1,0:T(8,128)(2,1)S(1)}, u32[]{:S(2)}, u32[]{:S(2)}) %collective-permute-start.5) | collective-permute-done | bytes 163872 | tf_op jit(solution)/shard_map/ppermute | solution.py:544
  23.1 2.9 %collective-permute-start.7 = (bf16[3,160,512]{2,1,0:T(8,128)(2,1)}, bf16[3,160,512]{2,1,0:T(8,128)(2,1)}, u32[]{:S(2)}, u32[]{:S(2)}) collective-permute-start(bf16[3,160,512]{2,1,0:T(8,128)(2,1)} %pad_maximum_fusion.p0), channel_id=1, source_target_pairs={{0,2},{2,0},{4,6},{6,4},{1,3},{3,1},{5,7},{7,5},{8,10},{10,8},{12,... | collective-permute-start | bytes 1474568 | tf_op jit(solution)/shard_map/ppermute | solution.py:548
  26.1 3.9 %collective-permute-start.13 = (bf16[192,1280]{1,0:T(8,128)(2,1)S(1)}, bf16[192,1280]{1,0:T(8,128)(2,1)}, u32[]{:S(2)}, u32[]{:S(2)}) collective-permute-start(bf16[192,1280]{1,0:T(8,128)(2,1)S(1)} %get-tuple-element.65), channel_id=1, source_target_pairs={{0,24},{8,16},{16,8},{24,0},{1,25},{9,17},{17,9},{25,1},{2,26},{10... | collective-permute-start | bytes 1474568 | tf_op jit(solution)/shard_map/ppermute | solution.py:549
  31.1 4.8 %attend_cached.1 = (f32[4,2,48,16,128]{4,3,2,1,0:T(8,128)S(1)}, f32[4,48,16,128]{3,2,1,0:T(8,128)S(1)}) custom-call(s32[4]{0:T(128)S(1)} %copy-done.13, bf16[4,48,32,128]{3,2,1,0:T(8,128)(2,1)S(1)} %copy-done.2, bf16[4,4,192,128]{3,2,1,0:T(8,128)(2,1)S(1)} %copy-done.14, bf16[4,4,192,128]{3,2,1,0:T(8,128)(2,1)S(1)} %copy-done.15), custom_call_target="tpu_custom_call" | custom-call | flops 4000000000 | bytes 12582912 | tf_op jit(solution)/shard_map/attend_cached/pallas_call | solution.py:421
  38.3 5.1 %collective-permute-done.13.da = bf16[192,1280]{1,0:T(8,128)(2,1)} collective-permute-done((bf16[192,1280]{1,0:T(8,128)(2,1)S(1)}, bf16[192,1280]{1,0:T(8,128)(2,1)}, u32[]{:S(2)}, u32[]{:S(2)}) %collective-permute-start.13) | collective-permute-done | bytes 491552 | tf_op jit(solution)/shard_map/ppermute | solution.py:549
  43.4 6.7 %collective-permute-start.10 = (bf16[160,512]{1,0:T(8,128)(2,1)S(1)}, bf16[160,512]{1,0:T(8,128)(2,1)}, u32[]{:S(2)}, u32[]{:S(2)}) collective-permute-start(bf16[160,512]{1,0:T(8,128)(2,1)S(1)} %collective-permute-done.3.o2), channel_id=1, source_target_pairs={{4,6},{2,0},{5,7},{3,1},{12,14},{10,8},{13,15},{11,9},{20,22},{18,... | collective-permute-start | bytes 491528 | tf_op jit(solution)/shard_map/ppermute | solution.py:554
  50.1 3.0 %collective-permute-done.10.oe = bf16[160,512]{1,0:T(8,128)(2,1)} collective-permute-done((bf16[160,512]{1,0:T(8,128)(2,1)S(1)}, bf16[160,512]{1,0:T(8,128)(2,1)}, u32[]{:S(2)}, u32[]{:S(2)}) %collective-permute-start.10) | collective-permute-done | bytes 163872 | tf_op jit(solution)/shard_map/ppermute | solution.py:554
  53.4 4.8 %collective-permute-start.16 = (bf16[3,160,512]{2,1,0:T(8,128)(2,1)}, bf16[3,160,512]{2,1,0:T(8,128)(2,1)}, u32[]{:S(2)}, u32[]{:S(2)}) collective-permute-start(bf16[3,160,512]{2,1,0:T(8,128)(2,1)} %collective-permute-done.6.p2), channel_id=1, source_target_pairs={{4,6},{2,0},{5,7},{3,1},{12,14},{10,8},{13,15},{11,9},{20,22},{18,... | collective-permute-start | bytes 1474568 | tf_op jit(solution)/shard_map/ppermute | solution.py:556
  58.2 1.9 %collective-permute-start.15 = (bf16[3,160,512]{2,1,0:T(8,128)(2,1)}, bf16[3,160,512]{2,1,0:T(8,128)(2,1)}, u32[]{:S(2)}, u32[]{:S(2)}) collective-permute-start(bf16[3,160,512]{2,1,0:T(8,128)(2,1)} %pad_maximum_fusion.p0), channel_id=1, source_target_pairs={{2,4},{4,2},{3,5},{5,3},{10,12},{12,10},{11,13},{13,11},{18,20},{2... | collective-permute-start | bytes 1474568 | tf_op jit(solution)/shard_map/ppermute | solution.py:557
  61.4 1.6 %collective-permute-done.11 = s32[4]{0:T(128)S(1)} collective-permute-done((s32[4]{0:T(128)S(1)}, s32[4]{0:T(128)S(1)}, u32[]{:S(2)}, u32[]{:S(2)}) %collective-permute-start.11) | collective-permute-done | bytes 48 | tf_op jit(solution)/shard_map/ppermute | solution.py:558
  64.1 2.0 %collective-permute-done.14.db = bf16[192,1280]{1,0:T(8,128)(2,1)} collective-permute-done((bf16[192,1280]{1,0:T(8,128)(2,1)}, bf16[192,1280]{1,0:T(8,128)(2,1)}, u32[]{:S(2)}, u32[]{:S(2)}) %collective-permute-start.14) | collective-permute-done | bytes 491552 | tf_op jit(solution)/shard_map/ppermute | solution.py:553
  66.1 1.5 %collective-permute-done.16.pe = bf16[3,160,512]{2,1,0:T(8,128)(2,1)} collective-permute-done((bf16[3,160,512]{2,1,0:T(8,128)(2,1)}, bf16[3,160,512]{2,1,0:T(8,128)(2,1)}, u32[]{:S(2)}, u32[]{:S(2)}) %collective-permute-start.16) | collective-permute-done | bytes 491552 | tf_op jit(solution)/shard_map/ppermute | solution.py:556
  67.6 4.6 %collective-permute-done.15.pm = bf16[3,160,512]{2,1,0:T(8,128)(2,1)} collective-permute-done((bf16[3,160,512]{2,1,0:T(8,128)(2,1)}, bf16[3,160,512]{2,1,0:T(8,128)(2,1)}, u32[]{:S(2)}, u32[]{:S(2)}) %collective-permute-start.15) | collective-permute-done | bytes 491552 | tf_op jit(solution)/shard_map/ppermute | solution.py:557
  72.2 1.5 %copy-done.1 = bf16[4,48,5120]{2,1,0:T(8,128)(2,1)S(1)} copy-done((bf16[4,48,5120]{2,1,0:T(8,128)(2,1)S(1)}, bf16[4,48,5120]{2,1,0:T(8,128)(2,1)}, u32[]{:S(2)}) %copy-start.1) | copy-done | bytes 1966104
  73.8 5.2 %project.1 = (f32[2,192,512]{2,1,0:T(8,128)S(1)}, f32[2,192,512]{2,1,0:T(8,128)S(1)}) custom-call(bf16[192,5120]{1,0:T(8,128)(2,1)S(1)} %bitcast.45, bf16[2,192,1280]{2,1,0:T(8,128)(2,1)} %collective-permute-done.12.c, bf16[192,1280]{1,0:T(8,128)(2,1)} %collective-permute-done.8.xa, bf16[192,1280]{1,0:T(8,128)(2,1)} %collective-permute-done.9.xb, ...), custom_call_target="tpu_custom_call" | custom-call | flops 1 | bytes 1 | tf_op jit(solution)/shard_map/project/pallas_call | solution.py:340
  79.0 1.9 %collective-permute-start.17 = (f32[2,192,512]{2,1,0:T(8,128)S(1)}, f32[2,192,512]{2,1,0:T(8,128)S(1)}, u32[]{:S(2)}, u32[]{:S(2)}) collective-permute-start(f32[2,192,512]{2,1,0:T(8,128)S(1)} %get-tuple-element.75), channel_id=1, source_target_pairs={{0,8},{8,0},{16,24},{24,16},{1,9},{9,1},{17,25},{25,17},{2,10},{10... | collective-permute-start | bytes 2359304 | tf_op jit(solution)/shard_map/ppermute | solution.py:572
  80.9 1.9 %collective-permute-done.17.crossed_ref = f32[2,192,512]{2,1,0:T(8,128)S(1)} collective-permute-done((f32[2,192,512]{2,1,0:T(8,128)S(1)}, f32[2,192,512]{2,1,0:T(8,128)S(1)}, u32[]{:S(2)}, u32[]{:S(2)}) %collective-permute-start.17) | collective-permute-done | bytes 786464 | tf_op jit(solution)/shard_map/ppermute | solution.py:572
  85.2 1.4 %copy-done.3 = bf16[4,48,32,128]{3,2,1,0:T(8,128)(2,1)S(1)} copy-done((bf16[4,48,32,128]{3,2,1,0:T(8,128)(2,1)S(1)}, bf16[4,48,32,128]{3,2,1,0:T(8,128)(2,1)}, u32[]{:S(2)}) %copy-start.3) | copy-done | bytes 1572888
  86.6 1.4 %copy-done.5 = f32[4,48,16,128]{3,2,1,0:T(8,128)S(1)} copy-done((f32[4,48,16,128]{3,2,1,0:T(8,128)S(1)}, f32[4,48,16,128]{3,2,1,0:T(8,128)}, u32[]{:S(2)}) %copy-start.5) | copy-done | bytes 1572888
  88.0 3.7 %finish.2 = (bf16[4,48,2,512]{3,2,1,0:T(2,128)(2,1)}, bf16[4,48,32,128]{3,2,1,0:T(8,128)(2,1)}) custom-call(s32[4]{0:T(128)S(1)} %copy-done.11, s32[1]{0:T(128)} %bitcast.29.place_ref, bf16[192,512]{1,0:T(8,128)(2,1)S(1)} %get-tuple-element.78.kv_ref, bf16[4,48,32,128]{3,2,1,0:T(8,128)(2,1)S(1)} %copy-done.3, ...), custom_call_target="tpu_custom_call" | custom-call | flops 1 | bytes 1 | tf_op jit(solution)/shard_map/finish/pallas_call | solution.py:492
  91.7 3.7 %finish.3 = (bf16[4,48,2,512]{3,2,1,0:T(2,128)(2,1)}, bf16[4,48,32,128]{3,2,1,0:T(8,128)(2,1)}) custom-call(s32[4]{0:T(128)S(1)} %copy-done.11, s32[1]{0:T(128)} %bitcast.21.place_ref, bf16[192,512]{1,0:T(8,128)(2,1)S(1)} %collective-permute-done.18.kv_ref, bf16[4,48,32,128]{3,2,1,0:T(8,128)(2,1)S(1)} %copy-done.3, ...), custom_call_target="tpu_custom_call", output_to_operand_aliasing={{0}: (6, {}), {1}: (7, {})} | custom-call | flops 1 | bytes 1 | tf_op jit(solution)/shard_map/finish/pallas_call | solution.py:492
  (67 shorter events, 17.5 us)
Async XLA Ops:
  6.1 23.8 %copy-start.2 = (bf16[4,48,32,128]{3,2,1,0:T(8,128)(2,1)S(1)}, bf16[4,48,32,128]{3,2,1,0:T(8,128)(2,1)}, u32[]{:S(2)}) copy-start(bf16[4,48,32,128]{3,2,1,0:T(8,128)(2,1)} %q_ref.5) | copy-start | bytes 4718596
  6.1 23.8 %copy-start.13 = (s32[4]{0:T(128)S(1)}, s32[4]{0:T(128)}, u32[]{:S(2)}) copy-start(s32[4]{0:T(128)} %lengths.2) | copy-start | bytes 52
  6.1 23.8 %copy-start.14 = (bf16[4,4,192,128]{3,2,1,0:T(8,128)(2,1)S(1)}, bf16[4,4,192,128]{3,2,1,0:T(8,128)(2,1)}, u32[]{:S(2)}) copy-start(bf16[4,4,192,128]{3,2,1,0:T(8,128)(2,1)} %k_ref.1) | copy-start | bytes 2359300
  7.4 7.1 %collective-permute-start.3 = (bf16[160,512]{1,0:T(8,128)(2,1)S(1)}, bf16[160,512]{1,0:T(8,128)(2,1)S(1)}, u32[]{:S(2)}, u32[]{:S(2)}) collective-permute-start(bf16[160,512]{1,0:T(8,128)(2,1)S(1)} %copy-done.6), channel_id=1, source_target_pairs={{0,4},{4,0},{2,6},{6,2},{1,5},{5,1},{3,7},{7,3},{8,12},{12,8},{10,... | collective-permute-start | bytes 491528 | tf_op jit(solution)/shard_map/ppermute | solution.py:544
  7.4 8.5 %collective-permute-start.4 = (bf16[160,512]{1,0:T(8,128)(2,1)S(1)}, bf16[160,512]{1,0:T(8,128)(2,1)S(1)}, u32[]{:S(2)}, u32[]{:S(2)}) collective-permute-start(bf16[160,512]{1,0:T(8,128)(2,1)S(1)} %copy-done.6), channel_id=1, source_target_pairs={{0,2},{2,0},{4,6},{6,4},{1,3},{3,1},{5,7},{7,5},{8,10},{10,8},{12,... | collective-permute-start | bytes 491528 | tf_op jit(solution)/shard_map/ppermute | solution.py:544
  8.8 12.7 %collective-permute-start.5 = (bf16[160,512]{1,0:T(8,128)(2,1)S(1)}, bf16[160,512]{1,0:T(8,128)(2,1)S(1)}, u32[]{:S(2)}, u32[]{:S(2)}) collective-permute-start(bf16[160,512]{1,0:T(8,128)(2,1)S(1)} %copy-done.6), channel_id=1, source_target_pairs={{2,4},{4,2},{3,5},{5,3},{10,12},{12,10},{11,13},{13,11},{18,20},{2... | collective-permute-start | bytes 491528 | tf_op jit(solution)/shard_map/ppermute | solution.py:544
  12.0 10.2 %collective-permute-start = (bf16[160,512]{1,0:T(8,128)(2,1)}, bf16[160,512]{1,0:T(8,128)(2,1)S(1)}, u32[]{:S(2)}, u32[]{:S(2)}) collective-permute-start(bf16[160,512]{1,0:T(8,128)(2,1)} %get-tuple-element.47), channel_id=1, source_target_pairs={{0,16},{8,24},{16,0},{24,8},{1,17},{9,25},{17,1},{25,9},{2,18},{10... | collective-permute-start | bytes 491528 | tf_op jit(solution)/shard_map/ppermute | solution.py:539
  13.2 8.9 %collective-permute-start.1 = (bf16[160,512]{1,0:T(8,128)(2,1)S(1)}, bf16[160,512]{1,0:T(8,128)(2,1)S(1)}, u32[]{:S(2)}, u32[]{:S(2)}) collective-permute-start(bf16[160,512]{1,0:T(8,128)(2,1)S(1)} %copy-done.17), channel_id=1, source_target_pairs={{0,1},{1,0},{2,3},{3,2},{4,5},{5,4},{6,7},{7,6},{8,9},{9,8},{10,11... | collective-permute-start | bytes 491528 | tf_op jit(solution)/shard_map/ppermute | solution.py:540
  14.5 7.6 %collective-permute-start.2 = (bf16[160,512]{1,0:T(8,128)(2,1)S(1)}, bf16[160,512]{1,0:T(8,128)(2,1)S(1)}, u32[]{:S(2)}, u32[]{:S(2)}) collective-permute-start(bf16[160,512]{1,0:T(8,128)(2,1)S(1)} %copy-done.16), channel_id=1, source_target_pairs={{0,17},{1,16},{8,25},{9,24},{16,1},{17,0},{24,9},{25,8},{2,19},{3,... | collective-permute-start | bytes 491528 | tf_op jit(solution)/shard_map/ppermute | solution.py:541
  16.6 20.4 %collective-permute-start.8 = (bf16[192,1280]{1,0:T(8,128)(2,1)S(1)}, bf16[192,1280]{1,0:T(8,128)(2,1)}, u32[]{:S(2)}, u32[]{:S(2)}) collective-permute-start(bf16[192,1280]{1,0:T(8,128)(2,1)S(1)} %get-tuple-element.52), channel_id=1, source_target_pairs={{0,16},{8,24},{16,0},{24,8},{1,17},{9,25},{17,1},{25,9},{2,18},{10... | collective-permute-start | bytes 1474568 | tf_op jit(solution)/shard_map/ppermute | solution.py:545
  23.0 30.4 %collective-permute-start.6 = (bf16[3,160,512]{2,1,0:T(8,128)(2,1)}, bf16[3,160,512]{2,1,0:T(8,128)(2,1)}, u32[]{:S(2)}, u32[]{:S(2)}) collective-permute-start(bf16[3,160,512]{2,1,0:T(8,128)(2,1)} %pad_maximum_fusion.p0), channel_id=1, source_target_pairs={{0,4},{4,0},{2,6},{6,2},{1,5},{5,1},{3,7},{7,3},{8,12},{12,8},{10,... | collective-permute-start | bytes 1474568 | tf_op jit(solution)/shard_map/ppermute | solution.py:547
  23.1 30.3 %collective-permute-start.7 = (bf16[3,160,512]{2,1,0:T(8,128)(2,1)}, bf16[3,160,512]{2,1,0:T(8,128)(2,1)}, u32[]{:S(2)}, u32[]{:S(2)}) collective-permute-start(bf16[3,160,512]{2,1,0:T(8,128)(2,1)} %pad_maximum_fusion.p0), channel_id=1, source_target_pairs={{0,2},{2,0},{4,6},{6,4},{1,3},{3,1},{5,7},{7,5},{8,10},{10,8},{12,... | collective-permute-start | bytes 1474568 | tf_op jit(solution)/shard_map/ppermute | solution.py:548
  26.1 17.3 %collective-permute-start.13 = (bf16[192,1280]{1,0:T(8,128)(2,1)S(1)}, bf16[192,1280]{1,0:T(8,128)(2,1)}, u32[]{:S(2)}, u32[]{:S(2)}) collective-permute-start(bf16[192,1280]{1,0:T(8,128)(2,1)S(1)} %get-tuple-element.65), channel_id=1, source_target_pairs={{0,24},{8,16},{16,8},{24,0},{1,25},{9,17},{17,9},{25,1},{2,26},{10... | collective-permute-start | bytes 1474568 | tf_op jit(solution)/shard_map/ppermute | solution.py:549
  37.0 16.4 %collective-permute-start.9 = (bf16[192,1280]{1,0:T(8,128)(2,1)}, bf16[192,1280]{1,0:T(8,128)(2,1)}, u32[]{:S(2)}, u32[]{:S(2)}) collective-permute-start(bf16[192,1280]{1,0:T(8,128)(2,1)} %collective-permute-done.8.xa), channel_id=1, source_target_pairs={{0,1},{1,0},{2,3},{3,2},{4,5},{5,4},{6,7},{7,6},{8,9},{9,8},{10,11... | collective-permute-start | bytes 1474568 | tf_op jit(solution)/shard_map/ppermute | solution.py:552
  38.3 27.9 %collective-permute-start.12 = (bf16[2,192,1280]{2,1,0:T(8,128)(2,1)}, bf16[2,192,1280]{2,1,0:T(8,128)(2,1)}, u32[]{:S(2)}, u32[]{:S(2)}) collective-permute-start(bf16[2,192,1280]{2,1,0:T(8,128)(2,1)} %get-tuple-element.63), channel_id=1, source_target_pairs={{0,8},{8,0},{16,24},{24,16},{1,9},{9,1},{17,25},{25,17},{2,10},{10... | collective-permute-start | bytes 2949128 | tf_op jit(solution)/shard_map/ppermute | solution.py:550
  43.4 9.8 %collective-permute-start.10 = (bf16[160,512]{1,0:T(8,128)(2,1)S(1)}, bf16[160,512]{1,0:T(8,128)(2,1)}, u32[]{:S(2)}, u32[]{:S(2)}) collective-permute-start(bf16[160,512]{1,0:T(8,128)(2,1)S(1)} %collective-permute-done.3.o2), channel_id=1, source_target_pairs={{4,6},{2,0},{5,7},{3,1},{12,14},{10,8},{13,15},{11,9},{20,22},{18,... | collective-permute-start | bytes 491528 | tf_op jit(solution)/shard_map/ppermute | solution.py:554
  53.2 13.0 %collective-permute-start.14 = (bf16[192,1280]{1,0:T(8,128)(2,1)}, bf16[192,1280]{1,0:T(8,128)(2,1)}, u32[]{:S(2)}, u32[]{:S(2)}) collective-permute-start(bf16[192,1280]{1,0:T(8,128)(2,1)} %collective-permute-done.13.da), channel_id=1, source_target_pairs={{0,1},{1,0},{2,3},{3,2},{4,5},{5,4},{6,7},{7,6},{8,9},{9,8},{10,11... | collective-permute-start | bytes 1474568 | tf_op jit(solution)/shard_map/ppermute | solution.py:553
  53.4 14.2 %collective-permute-start.16 = (bf16[3,160,512]{2,1,0:T(8,128)(2,1)}, bf16[3,160,512]{2,1,0:T(8,128)(2,1)}, u32[]{:S(2)}, u32[]{:S(2)}) collective-permute-start(bf16[3,160,512]{2,1,0:T(8,128)(2,1)} %collective-permute-done.6.p2), channel_id=1, source_target_pairs={{4,6},{2,0},{5,7},{3,1},{12,14},{10,8},{13,15},{11,9},{20,22},{18,... | collective-permute-start | bytes 1474568 | tf_op jit(solution)/shard_map/ppermute | solution.py:556
  58.2 14.0 %collective-permute-start.15 = (bf16[3,160,512]{2,1,0:T(8,128)(2,1)}, bf16[3,160,512]{2,1,0:T(8,128)(2,1)}, u32[]{:S(2)}, u32[]{:S(2)}) collective-permute-start(bf16[3,160,512]{2,1,0:T(8,128)(2,1)} %pad_maximum_fusion.p0), channel_id=1, source_target_pairs={{2,4},{4,2},{3,5},{5,3},{10,12},{12,10},{11,13},{13,11},{18,20},{2... | collective-permute-start | bytes 1474568 | tf_op jit(solution)/shard_map/ppermute | solution.py:557
  60.1 2.9 %collective-permute-start.11 = (s32[4]{0:T(128)S(1)}, s32[4]{0:T(128)S(1)}, u32[]{:S(2)}, u32[]{:S(2)}) collective-permute-start(s32[4]{0:T(128)S(1)} %copy-done.13), channel_id=1, source_target_pairs={{0,16},{8,24},{16,0},{24,8},{1,17},{9,25},{17,1},{25,9},{2,18},{10... | collective-permute-start | bytes 56 | tf_op jit(solution)/shard_map/ppermute | solution.py:558
  63.2 9.0 %copy-start.10 = (bf16[160,512]{1,0:T(8,128)(2,1)S(1)}, bf16[160,512]{1,0:T(8,128)(2,1)}, u32[]{:S(2)}) copy-start(bf16[160,512]{1,0:T(8,128)(2,1)} %copy-done.9) | copy-start | bytes 491524
  66.1 16.7 %copy-start.12 = (bf16[128]{0:T(256)(128)(2,1)S(1)}, bf16[128]{0:T(256)(128)(2,1)}, u32[]{:S(2)}) copy-start(bf16[128]{0:T(256)(128)(2,1)} %param.15) | copy-start | bytes 772
  79.0 3.8 %collective-permute-start.17 = (f32[2,192,512]{2,1,0:T(8,128)S(1)}, f32[2,192,512]{2,1,0:T(8,128)S(1)}, u32[]{:S(2)}, u32[]{:S(2)}) collective-permute-start(f32[2,192,512]{2,1,0:T(8,128)S(1)} %get-tuple-element.75), channel_id=1, source_target_pairs={{0,8},{8,0},{16,24},{24,16},{1,9},{9,1},{17,25},{25,17},{2,10},{10... | collective-permute-start | bytes 2359304 | tf_op jit(solution)/shard_map/ppermute | solution.py:572
  84.0 7.8 %collective-permute-start.18 = (bf16[192,512]{1,0:T(8,128)(2,1)}, bf16[192,512]{1,0:T(8,128)(2,1)S(1)}, u32[]{:S(2)}, u32[]{:S(2)}) collective-permute-start(bf16[192,512]{1,0:T(8,128)(2,1)} %get-tuple-element.76), channel_id=1, source_target_pairs={{0,16},{8,24},{16,0},{24,8},{1,17},{9,25},{17,1},{25,9},{2,18},{10... | collective-permute-start | bytes 589832 | tf_op jit(solution)/shard_map/ppermute | solution.py:574
  (13 other events, 45.6 us)
